TPU v7x, 768 devices: a whole 4x8x12 slice. The times are simulated.
768 devices in a mesh: circ: 16 (over y_lo, x), axial: 24 (over z, y_hi), rad: 2 (over core).
Axes of the slice: x: 4, y: 8 (y_hi: 2, y_lo: 4; y = y_hi * 4 + y_lo), z: 12, core: 2. Of those that a mesh axis runs over, the one named last changes fastest.
Arguments:
- flow: float32 [6, 64, 192, 256], P(None, 'circ', 'axial', 'rad'), may hold values from -0.3 to 1.2, as said below
- inflow: float32 [6, 64, 256], replicated, may hold values from -0.3 to 1.2, as said below
- wall_kind: int32 [192, 2], replicated, may hold values from 0 to 1
Outputs:
- advanced: float32 [6, 64, 192, 256], P(None, 'circ', 'axial', 'rad')
Inputs may be any that keep to these rules, and one draw needn't show every extreme that they name: `flow`: density and pressure lie in 0.8 to 1.2, circumferential velocity in -0.3 to 0.3, axial velocity in 0.2 to 0.6, radial velocity in -0.2 to 0.2, turbulence variable in 0.2 to 1.0. `inflow`: components lie in the same ranges as those of flow.
All inputs are finite; a program needn't handle non-finite values.
Results may differ from a plain program's by a relative error of at most 0.0003.
Values sent between devices are 32-bit elements; how exact they have to be, the bound alone decides.
A program may use at most 32 MiB of HBM per device.

v0:
```python
from functools import reduce

import jax
import jax.numpy as jnp
from jax import lax
from jax.sharding import PartitionSpec as P

GAMMA = 1.4
STEP_SIZE = 0.15
LIMIT_EPS = 0.03
FIX_WIDTH = 0.2
PRODUCE = 0.1355
DESTROY = 3.24


def with_halo(cells, sides, width, closed):
    for axis, dim in sides:
        count = lax.axis_size(axis)
        ends = count if closed else count - 1
        head = lax.slice_in_dim(cells, 0, width, axis=dim)
        tail = lax.slice_in_dim(cells, cells.shape[dim] - width, cells.shape[dim], axis=dim)
        cells = jnp.concatenate(
            [
                lax.ppermute(tail, axis, [(i, (i + 1) % count) for i in range(ends)]),
                cells,
                lax.ppermute(head, axis, [((i + 1) % count, i) for i in range(ends)]),
            ],
            axis=dim,
        )
    return cells


def conserved(prim):
    density = prim[0]
    energy = prim[4] / (GAMMA - 1.0) + 0.5 * density * (
        prim[1] * prim[1] + prim[2] * prim[2] + prim[3] * prim[3]
    )
    return jnp.stack(
        [
            density,
            density * prim[1],
            density * prim[2],
            density * prim[3],
            energy,
            density * prim[5],
        ]
    )


def primitive(cons):
    density = cons[0]
    vel_c = cons[1] / density
    vel_a = cons[2] / density
    vel_r = cons[3] / density
    pressure = (GAMMA - 1.0) * (
        cons[4] - 0.5 * density * (vel_c * vel_c + vel_a * vel_a + vel_r * vel_r)
    )
    return jnp.stack([density, vel_c, vel_a, vel_r, pressure, cons[5] / density])


def reflect(cells, kinds):
    noslip = jnp.where(kinds == 1, -1.0, 1.0)[None, :, None]
    return jnp.stack(
        [cells[0], noslip * cells[1], noslip * cells[2], -cells[3], cells[4], noslip * cells[5]]
    )


def venkat(upper, lower, delta):
    bound = jnp.where(delta > 0.0, upper, lower)
    top = bound * bound + LIMIT_EPS + 2.0 * delta * bound
    bottom = bound * bound + 2.0 * delta * delta + bound * delta + LIMIT_EPS
    return top / bottom


def limited(extended):
    centre = extended[:, 1:-1, 1:-1, 1:-1]
    beside_all = [
        extended[:, 2:, 1:-1, 1:-1],
        extended[:, :-2, 1:-1, 1:-1],
        extended[:, 1:-1, 2:, 1:-1],
        extended[:, 1:-1, :-2, 1:-1],
        extended[:, 1:-1, 1:-1, 2:],
        extended[:, 1:-1, 1:-1, :-2],
    ]
    grads = [
        0.5 * (beside_all[0] - beside_all[1]),
        0.5 * (beside_all[2] - beside_all[3]),
        0.5 * (beside_all[4] - beside_all[5]),
    ]
    upper = reduce(jnp.maximum, beside_all, centre) - centre
    lower = reduce(jnp.minimum, beside_all, centre) - centre
    factor = jnp.ones_like(centre)
    for grad in grads:
        factor = jnp.minimum(factor, venkat(upper, lower, 0.5 * grad))
        factor = jnp.minimum(factor, venkat(upper, lower, -0.5 * grad))
    return (grads, [factor * grad for grad in grads])


def entropy_fix(speed):
    magnitude = jnp.abs(speed)
    return jnp.where(
        magnitude < FIX_WIDTH,
        (speed * speed + FIX_WIDTH * FIX_WIDTH) / (2.0 * FIX_WIDTH),
        magnitude,
    )


def physical(state, direction):
    density = state[0]
    pressure = state[4]
    velocity = [state[1], state[2], state[3]]
    normal = velocity[direction]
    enthalpy = GAMMA / (GAMMA - 1.0) * pressure / density + 0.5 * (
        velocity[0] * velocity[0] + velocity[1] * velocity[1] + velocity[2] * velocity[2]
    )
    moment = [
        density * velocity[comp] * normal + (pressure if comp == direction else 0.0)
        for comp in range(3)
    ]
    return (
        [density * normal] + moment + [density * enthalpy * normal, density * state[5] * normal],
        enthalpy,
    )


def roe_flux(left, right, direction):
    flux_left, enth_left = physical(left, direction)
    flux_right, enth_right = physical(right, direction)
    root_left = jnp.sqrt(left[0])
    root_right = jnp.sqrt(right[0])
    weight_left = root_left / (root_left + root_right)
    weight_right = root_right / (root_left + root_right)
    velocity = [weight_left * left[comp + 1] + weight_right * right[comp + 1] for comp in range(3)]
    enthalpy = weight_left * enth_left + weight_right * enth_right
    turbulent = weight_left * left[5] + weight_right * right[5]
    normal = velocity[direction]
    speed_sq = velocity[0] * velocity[0] + velocity[1] * velocity[1] + velocity[2] * velocity[2]
    sound_sq = (GAMMA - 1.0) * (enthalpy - 0.5 * speed_sq)
    sound = jnp.sqrt(sound_sq)
    dens_avg = root_left * root_right
    jump = right - left
    jump_vel = [jump[1], jump[2], jump[3]]
    jump_norm = jump_vel[direction]
    wave_slow = (jump[4] - dens_avg * sound * jump_norm) / (2.0 * sound_sq)
    wave_fast = (jump[4] + dens_avg * sound * jump_norm) / (2.0 * sound_sq)
    wave_mid = jump[0] - jump[4] / sound_sq
    slow = entropy_fix(normal - sound) * wave_slow
    middle = entropy_fix(normal)
    fast = entropy_fix(normal + sound) * wave_fast
    dissip = [slow + middle * wave_mid + fast]
    for comp in range(3):
        along = sound if comp == direction else 0.0
        shear = jump_vel[comp] - (jump_norm if comp == direction else 0.0)
        dissip.append(
            slow * (velocity[comp] - along)
            + middle * (wave_mid * velocity[comp] + dens_avg * shear)
            + fast * (velocity[comp] + along)
        )
    inner = velocity[0] * jump_vel[0] + velocity[1] * jump_vel[1] + velocity[2] * jump_vel[2]
    dissip.append(
        slow * (enthalpy - sound * normal)
        + middle * (wave_mid * 0.5 * speed_sq + dens_avg * (inner - normal * jump_norm))
        + fast * (enthalpy + sound * normal)
    )
    dissip.append((slow + fast) * turbulent + middle * (wave_mid * turbulent + dens_avg * jump[5]))
    return jnp.stack(
        [0.5 * (flux_left[comp] + flux_right[comp]) - 0.5 * dissip[comp] for comp in range(6)]
    )


def divergence(line, slope, direction, axis):
    count = line.shape[axis] - 2
    left = lax.slice_in_dim(line, 0, count + 1, axis=axis) + 0.5 * lax.slice_in_dim(
        slope, 0, count + 1, axis=axis
    )
    right = lax.slice_in_dim(line, 1, count + 2, axis=axis) - 0.5 * lax.slice_in_dim(
        slope, 1, count + 2, axis=axis
    )
    flux = roe_flux(left, right, direction)
    return lax.slice_in_dim(flux, 1, count + 1, axis=axis) - lax.slice_in_dim(
        flux, 0, count, axis=axis
    )


def source_term(prim, grads, distance):
    omega_c = grads[1][3] - grads[2][2]
    omega_a = grads[2][1] - grads[0][3]
    omega_r = grads[0][2] - grads[1][1]
    vorticity = jnp.sqrt(omega_c * omega_c + omega_a * omega_a + omega_r * omega_r)
    ratio = prim[5] / distance
    return PRODUCE * vorticity * prim[0] * prim[5] - DESTROY * prim[0] * ratio * ratio


def body(flow, inflow, wall_kind):
    cells_c = flow.shape[1]
    cells_a = flow.shape[2]
    cells_r = flow.shape[3]
    depth = 1
    place_circ = lax.axis_index("circ")
    place_axial = lax.axis_index("axial")
    place_rad = lax.axis_index("rad")
    last_axial = lax.axis_size("axial") - 1
    last_rad = lax.axis_size("rad") - 1
    total_axial = cells_a * lax.axis_size("axial")
    total_rad = cells_r * lax.axis_size("rad")
    rolled = jnp.roll(inflow, depth - place_circ * cells_c, axis=1)[:, : cells_c + 2 * depth]
    edged = jnp.concatenate(
        [rolled[:, :, :1]] * depth + [rolled] + [rolled[:, :, -1:]] * depth, axis=2
    )
    inflow_window = lax.dynamic_slice_in_dim(edged, place_rad * cells_r, cells_r + 2 * depth, 2)
    stations = jnp.clip(
        place_axial * cells_a - depth + jnp.arange(cells_a + 2 * depth), 0, total_axial - 1
    )
    kinds = wall_kind[stations]
    radial = place_rad * cells_r + jnp.arange(cells_r)
    distance = (jnp.minimum(radial, total_rad - 1 - radial) + 1).astype(jnp.float32)

    def extend(prim):
        around_circ = with_halo(prim, (("circ", 1),), depth, True)
        extended = with_halo(around_circ, (("axial", 2), ("rad", 3)), depth, False)
        entry_rows = inflow_window[:, :, None, :]
        exit_rows = extended[:, :, cells_a + depth - 1 : cells_a + depth]
        before_axial = jnp.where(place_axial == 0, entry_rows, extended[:, :, :depth])
        after_axial = jnp.where(
            place_axial == last_axial, exit_rows, extended[:, :, cells_a + depth :]
        )
        extended = jnp.concatenate(
            [before_axial, extended[:, :, depth : cells_a + depth], after_axial], axis=2
        )
        hub_ghost = reflect(extended[:, :, :, depth : 2 * depth][:, :, :, ::-1], kinds[:, 0])
        casing_ghost = reflect(
            extended[:, :, :, cells_r : cells_r + depth][:, :, :, ::-1], kinds[:, 1]
        )
        before_rad = jnp.where(place_rad == 0, hub_ghost, extended[:, :, :, :depth])
        after_rad = jnp.where(
            place_rad == last_rad, casing_ghost, extended[:, :, :, cells_r + depth :]
        )
        return jnp.concatenate(
            [before_rad, extended[:, :, :, depth : cells_r + depth], after_rad], axis=3
        )

    def residual(prim):
        extended = extend(prim)
        grads, slopes = limited(extended)
        slope_circ = with_halo(slopes[0], (("circ", 1),), 1, True)
        paired = with_halo(jnp.stack([slopes[1], slopes[2]]), (("axial", 3), ("rad", 4)), 1, False)
        slope_axial = paired[0][:, :, :, 1:-1]
        slope_radial = paired[1][:, :, 1:-1, :]
        line_circ = extended[
            :, depth - 1 : depth + cells_c + 1, depth : depth + cells_a, depth : depth + cells_r
        ]
        line_axial = extended[
            :, depth : depth + cells_c, depth - 1 : depth + cells_a + 1, depth : depth + cells_r
        ]
        line_radial = extended[
            :, depth : depth + cells_c, depth : depth + cells_a, depth - 1 : depth + cells_r + 1
        ]
        total = divergence(line_circ, slope_circ, 0, 1)
        total = total + divergence(line_axial, slope_axial, 1, 2)
        total = total + divergence(line_radial, slope_radial, 2, 3)
        source = source_term(prim, grads, distance)
        return jnp.concatenate([-total[:5], (-total[5] + source)[None]], axis=0)

    start = conserved(flow)
    section_one = start + STEP_SIZE * residual(flow)
    section_two = section_one + STEP_SIZE * residual(primitive(section_one))
    return 0.5 * start + 0.5 * section_two


def solution(mesh):
    in_specs = (P(None, "circ", "axial", "rad"), P(), P())
    out_specs = P(None, "circ", "axial", "rad")
    return jax.shard_map(body, mesh=mesh, in_specs=in_specs, out_specs=out_specs, check_vma=False)
```

profile of v0, /device:TPU:192, one launch (start us, length us, event | category | flops | bytes accessed | tf_op | source)
XLA Modules:
  0.0 132.9 jit_solution(12841946658903227108)
XLA Ops:
  0.8 7.7 %collective-permute-start.1 = (f32[6,1,8,128]{3,2,1,0:T(8,128)S(1)}, f32[6,1,8,128]{3,2,1,0:T(8,128)S(1)}, u32[]{:S(2)}, u32[]{:S(2)}) collective-permute-start(f32[6,1,8,128]{3,2,1,0:T(8,128)S(1)} %get-tuple-element.186), channel_id=1, source_target_pairs={{48,0},{96,48},{144,96},{192,144},{240,192},{288,240},{336,288},{3... | collective-permute-start | bytes 73736 | tf_op jit(solution)/shard_map/ppermute | solution.py:26
  8.5 1.9 %collective-permute-start = (f32[6,1,8,128]{3,2,1,0:T(8,128)S(1)}, f32[6,1,8,128]{3,2,1,0:T(8,128)S(1)}, u32[]{:S(2)}, u32[]{:S(2)}) collective-permute-start(f32[6,1,8,128]{3,2,1,0:T(8,128)S(1)} %get-tuple-element.187), channel_id=1, source_target_pairs={{0,48},{48,96},{96,144},{144,192},{192,240},{240,288},{288,336},{3... | collective-permute-start | bytes 73736 | tf_op jit(solution)/shard_map/ppermute | solution.py:24
  13.3 4.8 %collective-permute-done = f32[6,1,8,128]{3,2,1,0:T(8,128)S(1)} collective-permute-done((f32[6,1,8,128]{3,2,1,0:T(8,128)S(1)}, f32[6,1,8,128]{3,2,1,0:T(8,128)S(1)}, u32[]{:S(2)}, u32[]{:S(2)}) %collective-permute-start) | collective-permute-done | bytes 24608 | tf_op jit(solution)/shard_map/ppermute | solution.py:24
  18.2 5.0 %collective-permute-start.2 = (f32[6,6,1,128]{3,2,1,0:T(1,128)S(1)}, f32[6,6,1,128]{3,2,1,0:T(1,128)S(1)}, u32[]{:S(2)}, u32[]{:S(2)}) collective-permute-start(f32[6,6,1,128]{3,2,1,0:T(1,128)S(1)} %get-tuple-element.169), channel_id=1, source_target_pairs={{0,2},{2,4},{4,6},{6,8},{8,10},{10,12},{12,14},{14,16},{16,18},{18... | collective-permute-start | bytes 55304 | tf_op jit(solution)/shard_map/ppermute | solution.py:24
  23.3 5.6 %collective-permute-start.3 = (f32[6,6,1,128]{3,2,1,0:T(1,128)S(1)}, f32[6,6,1,128]{3,2,1,0:T(1,128)S(1)}, u32[]{:S(2)}, u32[]{:S(2)}) collective-permute-start(f32[6,6,1,128]{3,2,1,0:T(1,128)S(1)} %get-tuple-element.170), channel_id=1, source_target_pairs={{2,0},{4,2},{6,4},{8,6},{10,8},{12,10},{14,12},{16,14},{18,16},{20... | collective-permute-start | bytes 55304 | tf_op jit(solution)/shard_map/ppermute | solution.py:26
  29.1 3.8 %collective-permute-done.3 = f32[6,6,1,128]{3,2,1,0:T(1,128)S(1)} collective-permute-done((f32[6,6,1,128]{3,2,1,0:T(1,128)S(1)}, f32[6,6,1,128]{3,2,1,0:T(1,128)S(1)}, u32[]{:S(2)}, u32[]{:S(2)}) %collective-permute-start.3) | collective-permute-done | bytes 18464 | tf_op jit(solution)/shard_map/ppermute | solution.py:26
  33.0 1.3 collective-permute-start.4
  34.4 1.3 collective-permute-start.5
  35.7 2.1 %collective-permute-done.5 = f32[6,6,10,1]{3,2,1,0:T(8,128)S(1)} collective-permute-done((f32[6,6,10,1]{3,2,1,0:T(8,128)S(1)}, f32[6,6,10,1]{3,2,1,0:T(8,128)S(1)}, u32[]{:S(2)}, u32[]{:S(2)}) %collective-permute-start.5) | collective-permute-done | bytes 1472 | tf_op jit(solution)/shard_map/ppermute | solution.py:26
  40.4 9.8 %collective-permute-start.8 = (f32[2,6,4,1,128]{4,3,2,1,0:T(1,128)S(1)}, f32[2,6,4,1,128]{4,3,2,1,0:T(1,128)S(1)}, u32[]{:S(2)}, u32[]{:S(2)}) collective-permute-start(f32[2,6,4,1,128]{4,3,2,1,0:T(1,128)S(1)} %get-tuple-element.161), channel_id=1, source_target_pairs={{0,2},{2,4},{4,6},{6,8},{8,10},{10,12},{12,14},{14,16},{16,18},{18... | collective-permute-start | bytes 73736 | tf_op jit(solution)/shard_map/ppermute | solution.py:24
  50.3 1.9 %collective-permute-start.9 = (f32[2,6,4,1,128]{4,3,2,1,0:T(1,128)S(1)}, f32[2,6,4,1,128]{4,3,2,1,0:T(1,128)S(1)}, u32[]{:S(2)}, u32[]{:S(2)}) collective-permute-start(f32[2,6,4,1,128]{4,3,2,1,0:T(1,128)S(1)} %get-tuple-element.162), channel_id=1, source_target_pairs={{2,0},{4,2},{6,4},{8,6},{10,8},{12,10},{14,12},{16,14},{18,16},{20... | collective-permute-start | bytes 73736 | tf_op jit(solution)/shard_map/ppermute | solution.py:26
  52.2 3.1 %collective-permute-start.7 = (f32[6,1,8,128]{3,2,1,0:T(8,128)S(1)}, f32[6,1,8,128]{3,2,1,0:T(8,128)S(1)}, u32[]{:S(2)}, u32[]{:S(2)}) collective-permute-start(f32[6,1,8,128]{3,2,1,0:T(8,128)S(1)} %get-tuple-element.179), channel_id=1, source_target_pairs={{48,0},{96,48},{144,96},{192,144},{240,192},{288,240},{336,288},{3... | collective-permute-start | bytes 73736 | tf_op jit(solution)/shard_map/ppermute | solution.py:26
  55.3 2.8 %collective-permute-start.6 = (f32[6,1,8,128]{3,2,1,0:T(8,128)S(1)}, f32[6,1,8,128]{3,2,1,0:T(8,128)S(1)}, u32[]{:S(2)}, u32[]{:S(2)}) collective-permute-start(f32[6,1,8,128]{3,2,1,0:T(8,128)S(1)} %get-tuple-element.180), channel_id=1, source_target_pairs={{0,48},{48,96},{96,144},{144,192},{192,240},{240,288},{288,336},{3... | collective-permute-start | bytes 73736 | tf_op jit(solution)/shard_map/ppermute | solution.py:24
  58.1 2.1 %collective-permute-done.9 = f32[2,6,4,1,128]{4,3,2,1,0:T(1,128)S(1)} collective-permute-done((f32[2,6,4,1,128]{4,3,2,1,0:T(1,128)S(1)}, f32[2,6,4,1,128]{4,3,2,1,0:T(1,128)S(1)}, u32[]{:S(2)}, u32[]{:S(2)}) %collective-permute-start.9) | collective-permute-done | bytes 24608 | tf_op jit(solution)/shard_map/ppermute | solution.py:26
  60.4 1.3 collective-permute-start.10
  61.8 1.3 collective-permute-start.11
  63.1 1.8 %collective-permute-done.6 = f32[6,1,8,128]{3,2,1,0:T(8,128)S(1)} collective-permute-done((f32[6,1,8,128]{3,2,1,0:T(8,128)S(1)}, f32[6,1,8,128]{3,2,1,0:T(8,128)S(1)}, u32[]{:S(2)}, u32[]{:S(2)}) %collective-permute-start.6) | collective-permute-done | bytes 24608 | tf_op jit(solution)/shard_map/ppermute | solution.py:24
  67.7 4.9 %collective-permute-start.13 = (f32[6,1,8,128]{3,2,1,0:T(8,128)S(1)}, f32[6,1,8,128]{3,2,1,0:T(8,128)S(1)}, u32[]{:S(2)}, u32[]{:S(2)}) collective-permute-start(f32[6,1,8,128]{3,2,1,0:T(8,128)S(1)} %get-tuple-element.175), channel_id=1, source_target_pairs={{48,0},{96,48},{144,96},{192,144},{240,192},{288,240},{336,288},{3... | collective-permute-start | bytes 73736 | tf_op jit(solution)/shard_map/ppermute | solution.py:26
  72.6 1.9 %collective-permute-start.12 = (f32[6,1,8,128]{3,2,1,0:T(8,128)S(1)}, f32[6,1,8,128]{3,2,1,0:T(8,128)S(1)}, u32[]{:S(2)}, u32[]{:S(2)}) collective-permute-start(f32[6,1,8,128]{3,2,1,0:T(8,128)S(1)} %get-tuple-element.176), channel_id=1, source_target_pairs={{0,48},{48,96},{96,144},{144,192},{192,240},{240,288},{288,336},{3... | collective-permute-start | bytes 73736 | tf_op jit(solution)/shard_map/ppermute | solution.py:24
  74.6 7.8 %collective-permute-done.12 = f32[6,1,8,128]{3,2,1,0:T(8,128)S(1)} collective-permute-done((f32[6,1,8,128]{3,2,1,0:T(8,128)S(1)}, f32[6,1,8,128]{3,2,1,0:T(8,128)S(1)}, u32[]{:S(2)}, u32[]{:S(2)}) %collective-permute-start.12) | collective-permute-done | bytes 24608 | tf_op jit(solution)/shard_map/ppermute | solution.py:24
  82.4 7.7 %collective-permute-start.14 = (f32[6,6,1,128]{3,2,1,0:T(1,128)S(1)}, f32[6,6,1,128]{3,2,1,0:T(1,128)S(1)}, u32[]{:S(2)}, u32[]{:S(2)}) collective-permute-start(f32[6,6,1,128]{3,2,1,0:T(1,128)S(1)} %get-tuple-element.167), channel_id=1, source_target_pairs={{0,2},{2,4},{4,6},{6,8},{8,10},{10,12},{12,14},{14,16},{16,18},{18... | collective-permute-start | bytes 55304 | tf_op jit(solution)/shard_map/ppermute | solution.py:24
  90.1 2.9 %collective-permute-start.15 = (f32[6,6,1,128]{3,2,1,0:T(1,128)S(1)}, f32[6,6,1,128]{3,2,1,0:T(1,128)S(1)}, u32[]{:S(2)}, u32[]{:S(2)}) collective-permute-start(f32[6,6,1,128]{3,2,1,0:T(1,128)S(1)} %get-tuple-element.168), channel_id=1, source_target_pairs={{2,0},{4,2},{6,4},{8,6},{10,8},{12,10},{14,12},{16,14},{18,16},{20... | collective-permute-start | bytes 55304 | tf_op jit(solution)/shard_map/ppermute | solution.py:26
  93.0 6.6 %collective-permute-done.15 = f32[6,6,1,128]{3,2,1,0:T(1,128)S(1)} collective-permute-done((f32[6,6,1,128]{3,2,1,0:T(1,128)S(1)}, f32[6,6,1,128]{3,2,1,0:T(1,128)S(1)}, u32[]{:S(2)}, u32[]{:S(2)}) %collective-permute-start.15) | collective-permute-done | bytes 18464 | tf_op jit(solution)/shard_map/ppermute | solution.py:26
  99.9 1.3 collective-permute-start.16
  102.5 2.2 %collective-permute-done.17 = f32[6,6,10,1]{3,2,1,0:T(8,128)S(1)} collective-permute-done((f32[6,6,10,1]{3,2,1,0:T(8,128)S(1)}, f32[6,6,10,1]{3,2,1,0:T(8,128)S(1)}, u32[]{:S(2)}, u32[]{:S(2)}) %collective-permute-start.17) | collective-permute-done | bytes 1472 | tf_op jit(solution)/shard_map/ppermute | solution.py:26
  107.3 7.1 %collective-permute-start.20 = (f32[2,6,4,1,128]{4,3,2,1,0:T(1,128)S(1)}, f32[2,6,4,1,128]{4,3,2,1,0:T(1,128)S(1)}, u32[]{:S(2)}, u32[]{:S(2)}) collective-permute-start(f32[2,6,4,1,128]{4,3,2,1,0:T(1,128)S(1)} %get-tuple-element.155), channel_id=1, source_target_pairs={{0,2},{2,4},{4,6},{6,8},{8,10},{10,12},{12,14},{14,16},{16,18},{18... | collective-permute-start | bytes 73736 | tf_op jit(solution)/shard_map/ppermute | solution.py:24
  114.5 3.5 %collective-permute-start.21 = (f32[2,6,4,1,128]{4,3,2,1,0:T(1,128)S(1)}, f32[2,6,4,1,128]{4,3,2,1,0:T(1,128)S(1)}, u32[]{:S(2)}, u32[]{:S(2)}) collective-permute-start(f32[2,6,4,1,128]{4,3,2,1,0:T(1,128)S(1)} %get-tuple-element.156), channel_id=1, source_target_pairs={{2,0},{4,2},{6,4},{8,6},{10,8},{12,10},{14,12},{16,14},{18,16},{20... | collective-permute-start | bytes 73736 | tf_op jit(solution)/shard_map/ppermute | solution.py:26
  118.0 1.9 %collective-permute-start.19 = (f32[6,1,8,128]{3,2,1,0:T(8,128)S(1)}, f32[6,1,8,128]{3,2,1,0:T(8,128)S(1)}, u32[]{:S(2)}, u32[]{:S(2)}) collective-permute-start(f32[6,1,8,128]{3,2,1,0:T(8,128)S(1)} %get-tuple-element.171), channel_id=1, source_target_pairs={{48,0},{96,48},{144,96},{192,144},{240,192},{288,240},{336,288},{3... | collective-permute-start | bytes 73736 | tf_op jit(solution)/shard_map/ppermute | solution.py:26
  119.9 3.9 %collective-permute-start.18 = (f32[6,1,8,128]{3,2,1,0:T(8,128)S(1)}, f32[6,1,8,128]{3,2,1,0:T(8,128)S(1)}, u32[]{:S(2)}, u32[]{:S(2)}) collective-permute-start(f32[6,1,8,128]{3,2,1,0:T(8,128)S(1)} %get-tuple-element.172), channel_id=1, source_target_pairs={{0,48},{48,96},{96,144},{144,192},{192,240},{240,288},{288,336},{3... | collective-permute-start | bytes 73736 | tf_op jit(solution)/shard_map/ppermute | solution.py:24
  124.4 1.3 collective-permute-start.22
  125.7 1.5 %collective-permute-start.23 = (f32[2,6,4,10,1]{4,3,2,1,0:T(8,128)S(1)}, f32[2,6,4,10,1]{4,3,2,1,0:T(8,128)S(1)}, u32[]{:S(2)}, u32[]{:S(2)}) collective-permute-start(f32[2,6,4,10,1]{4,3,2,1,0:T(8,128)S(1)} %get-tuple-element.145), channel_id=1, source_target_pairs={{1,0},{3,2},{5,4},{7,6},{9,8},{11,10},{13,12},{15,14},{17,16},{19,... | collective-permute-start | bytes 5768 | tf_op jit(solution)/shard_map/ppermute | solution.py:26
  127.2 2.4 %collective-permute-done.18 = f32[6,1,8,128]{3,2,1,0:T(8,128)S(1)} collective-permute-done((f32[6,1,8,128]{3,2,1,0:T(8,128)S(1)}, f32[6,1,8,128]{3,2,1,0:T(8,128)S(1)}, u32[]{:S(2)}, u32[]{:S(2)}) %collective-permute-start.18) | collective-permute-done | bytes 24608 | tf_op jit(solution)/shard_map/ppermute | solution.py:24
  (143 shorter events, 17.2 us)
Async XLA Ops:
  0.0 10.5 %copy-start = (f32[6,4,8,128]{3,2,1,0:T(8,128)S(1)}, f32[6,4,8,128]{3,2,1,0:T(8,128)}, u32[]{:S(2)}) copy-start(f32[6,4,8,128]{3,2,1,0:T(8,128)} %param.3) | copy-start | bytes 294916
  0.8 17.4 %collective-permute-start.1 = (f32[6,1,8,128]{3,2,1,0:T(8,128)S(1)}, f32[6,1,8,128]{3,2,1,0:T(8,128)S(1)}, u32[]{:S(2)}, u32[]{:S(2)}) collective-permute-start(f32[6,1,8,128]{3,2,1,0:T(8,128)S(1)} %get-tuple-element.186), channel_id=1, source_target_pairs={{48,0},{96,48},{144,96},{192,144},{240,192},{288,240},{336,288},{3... | collective-permute-start | bytes 73736 | tf_op jit(solution)/shard_map/ppermute | solution.py:26
  8.5 9.6 %collective-permute-start = (f32[6,1,8,128]{3,2,1,0:T(8,128)S(1)}, f32[6,1,8,128]{3,2,1,0:T(8,128)S(1)}, u32[]{:S(2)}, u32[]{:S(2)}) collective-permute-start(f32[6,1,8,128]{3,2,1,0:T(8,128)S(1)} %get-tuple-element.187), channel_id=1, source_target_pairs={{0,48},{48,96},{96,144},{144,192},{192,240},{240,288},{288,336},{3... | collective-permute-start | bytes 73736 | tf_op jit(solution)/shard_map/ppermute | solution.py:24
  12.0 0.7 copy-start.1
  18.2 10.9 %collective-permute-start.2 = (f32[6,6,1,128]{3,2,1,0:T(1,128)S(1)}, f32[6,6,1,128]{3,2,1,0:T(1,128)S(1)}, u32[]{:S(2)}, u32[]{:S(2)}) collective-permute-start(f32[6,6,1,128]{3,2,1,0:T(1,128)S(1)} %get-tuple-element.169), channel_id=1, source_target_pairs={{0,2},{2,4},{4,6},{6,8},{8,10},{10,12},{12,14},{14,16},{16,18},{18... | collective-permute-start | bytes 55304 | tf_op jit(solution)/shard_map/ppermute | solution.py:24
  23.3 9.6 %collective-permute-start.3 = (f32[6,6,1,128]{3,2,1,0:T(1,128)S(1)}, f32[6,6,1,128]{3,2,1,0:T(1,128)S(1)}, u32[]{:S(2)}, u32[]{:S(2)}) collective-permute-start(f32[6,6,1,128]{3,2,1,0:T(1,128)S(1)} %get-tuple-element.170), channel_id=1, source_target_pairs={{2,0},{4,2},{6,4},{8,6},{10,8},{12,10},{14,12},{16,14},{18,16},{20... | collective-permute-start | bytes 55304 | tf_op jit(solution)/shard_map/ppermute | solution.py:26
  33.0 2.6 %collective-permute-start.4 = (f32[6,6,10,1]{3,2,1,0:T(8,128)S(1)}, f32[6,6,10,1]{3,2,1,0:T(8,128)S(1)}, u32[]{:S(2)}, u32[]{:S(2)}) collective-permute-start(f32[6,6,10,1]{3,2,1,0:T(8,128)S(1)} %get-tuple-element.152), channel_id=1, source_target_pairs={{0,1},{2,3},{4,5},{6,7},{8,9},{10,11},{12,13},{14,15},{16,17},{18,... | collective-permute-start | bytes 4328 | tf_op jit(solution)/shard_map/ppermute | solution.py:24
  34.4 3.5 %collective-permute-start.5 = (f32[6,6,10,1]{3,2,1,0:T(8,128)S(1)}, f32[6,6,10,1]{3,2,1,0:T(8,128)S(1)}, u32[]{:S(2)}, u32[]{:S(2)}) collective-permute-start(f32[6,6,10,1]{3,2,1,0:T(8,128)S(1)} %get-tuple-element.153), channel_id=1, source_target_pairs={{1,0},{3,2},{5,4},{7,6},{9,8},{11,10},{13,12},{15,14},{17,16},{19,... | collective-permute-start | bytes 4328 | tf_op jit(solution)/shard_map/ppermute | solution.py:26
  40.4 17.7 %collective-permute-start.8 = (f32[2,6,4,1,128]{4,3,2,1,0:T(1,128)S(1)}, f32[2,6,4,1,128]{4,3,2,1,0:T(1,128)S(1)}, u32[]{:S(2)}, u32[]{:S(2)}) collective-permute-start(f32[2,6,4,1,128]{4,3,2,1,0:T(1,128)S(1)} %get-tuple-element.161), channel_id=1, source_target_pairs={{0,2},{2,4},{4,6},{6,8},{8,10},{10,12},{12,14},{14,16},{16,18},{18... | collective-permute-start | bytes 73736 | tf_op jit(solution)/shard_map/ppermute | solution.py:24
  50.3 9.9 %collective-permute-start.9 = (f32[2,6,4,1,128]{4,3,2,1,0:T(1,128)S(1)}, f32[2,6,4,1,128]{4,3,2,1,0:T(1,128)S(1)}, u32[]{:S(2)}, u32[]{:S(2)}) collective-permute-start(f32[2,6,4,1,128]{4,3,2,1,0:T(1,128)S(1)} %get-tuple-element.162), channel_id=1, source_target_pairs={{2,0},{4,2},{6,4},{8,6},{10,8},{12,10},{14,12},{16,14},{18,16},{20... | collective-permute-start | bytes 73736 | tf_op jit(solution)/shard_map/ppermute | solution.py:26
  52.2 10.8 %collective-permute-start.7 = (f32[6,1,8,128]{3,2,1,0:T(8,128)S(1)}, f32[6,1,8,128]{3,2,1,0:T(8,128)S(1)}, u32[]{:S(2)}, u32[]{:S(2)}) collective-permute-start(f32[6,1,8,128]{3,2,1,0:T(8,128)S(1)} %get-tuple-element.179), channel_id=1, source_target_pairs={{48,0},{96,48},{144,96},{192,144},{240,192},{288,240},{336,288},{3... | collective-permute-start | bytes 73736 | tf_op jit(solution)/shard_map/ppermute | solution.py:26
  55.3 9.6 %collective-permute-start.6 = (f32[6,1,8,128]{3,2,1,0:T(8,128)S(1)}, f32[6,1,8,128]{3,2,1,0:T(8,128)S(1)}, u32[]{:S(2)}, u32[]{:S(2)}) collective-permute-start(f32[6,1,8,128]{3,2,1,0:T(8,128)S(1)} %get-tuple-element.180), channel_id=1, source_target_pairs={{0,48},{48,96},{96,144},{144,192},{192,240},{240,288},{288,336},{3... | collective-permute-start | bytes 73736 | tf_op jit(solution)/shard_map/ppermute | solution.py:24
  60.4 4.9 %collective-permute-start.10 = (f32[2,6,4,10,1]{4,3,2,1,0:T(8,128)S(1)}, f32[2,6,4,10,1]{4,3,2,1,0:T(8,128)S(1)}, u32[]{:S(2)}, u32[]{:S(2)}) collective-permute-start(f32[2,6,4,10,1]{4,3,2,1,0:T(8,128)S(1)} %get-tuple-element.146), channel_id=1, source_target_pairs={{0,1},{2,3},{4,5},{6,7},{8,9},{10,11},{12,13},{14,15},{16,17},{18,... | collective-permute-start | bytes 5768 | tf_op jit(solution)/shard_map/ppermute | solution.py:24
  61.8 3.6 %collective-permute-start.11 = (f32[2,6,4,10,1]{4,3,2,1,0:T(8,128)S(1)}, f32[2,6,4,10,1]{4,3,2,1,0:T(8,128)S(1)}, u32[]{:S(2)}, u32[]{:S(2)}) collective-permute-start(f32[2,6,4,10,1]{4,3,2,1,0:T(8,128)S(1)} %get-tuple-element.147), channel_id=1, source_target_pairs={{1,0},{3,2},{5,4},{7,6},{9,8},{11,10},{13,12},{15,14},{17,16},{19,... | collective-permute-start | bytes 5768 | tf_op jit(solution)/shard_map/ppermute | solution.py:26
  67.7 6.8 %collective-permute-start.13 = (f32[6,1,8,128]{3,2,1,0:T(8,128)S(1)}, f32[6,1,8,128]{3,2,1,0:T(8,128)S(1)}, u32[]{:S(2)}, u32[]{:S(2)}) collective-permute-start(f32[6,1,8,128]{3,2,1,0:T(8,128)S(1)} %get-tuple-element.175), channel_id=1, source_target_pairs={{48,0},{96,48},{144,96},{192,144},{240,192},{288,240},{336,288},{3... | collective-permute-start | bytes 73736 | tf_op jit(solution)/shard_map/ppermute | solution.py:26
  72.6 9.7 %collective-permute-start.12 = (f32[6,1,8,128]{3,2,1,0:T(8,128)S(1)}, f32[6,1,8,128]{3,2,1,0:T(8,128)S(1)}, u32[]{:S(2)}, u32[]{:S(2)}) collective-permute-start(f32[6,1,8,128]{3,2,1,0:T(8,128)S(1)} %get-tuple-element.176), channel_id=1, source_target_pairs={{0,48},{48,96},{96,144},{144,192},{192,240},{240,288},{288,336},{3... | collective-permute-start | bytes 73736 | tf_op jit(solution)/shard_map/ppermute | solution.py:24
  82.4 10.7 %collective-permute-start.14 = (f32[6,6,1,128]{3,2,1,0:T(1,128)S(1)}, f32[6,6,1,128]{3,2,1,0:T(1,128)S(1)}, u32[]{:S(2)}, u32[]{:S(2)}) collective-permute-start(f32[6,6,1,128]{3,2,1,0:T(1,128)S(1)} %get-tuple-element.167), channel_id=1, source_target_pairs={{0,2},{2,4},{4,6},{6,8},{8,10},{10,12},{12,14},{14,16},{16,18},{18... | collective-permute-start | bytes 55304 | tf_op jit(solution)/shard_map/ppermute | solution.py:24
  90.1 9.6 %collective-permute-start.15 = (f32[6,6,1,128]{3,2,1,0:T(1,128)S(1)}, f32[6,6,1,128]{3,2,1,0:T(1,128)S(1)}, u32[]{:S(2)}, u32[]{:S(2)}) collective-permute-start(f32[6,6,1,128]{3,2,1,0:T(1,128)S(1)} %get-tuple-element.168), channel_id=1, source_target_pairs={{2,0},{4,2},{6,4},{8,6},{10,8},{12,10},{14,12},{16,14},{18,16},{20... | collective-permute-start | bytes 55304 | tf_op jit(solution)/shard_map/ppermute | solution.py:26
  99.9 2.6 %collective-permute-start.16 = (f32[6,6,10,1]{3,2,1,0:T(8,128)S(1)}, f32[6,6,10,1]{3,2,1,0:T(8,128)S(1)}, u32[]{:S(2)}, u32[]{:S(2)}) collective-permute-start(f32[6,6,10,1]{3,2,1,0:T(8,128)S(1)} %get-tuple-element.150), channel_id=1, source_target_pairs={{0,1},{2,3},{4,5},{6,7},{8,9},{10,11},{12,13},{14,15},{16,17},{18,... | collective-permute-start | bytes 4328 | tf_op jit(solution)/shard_map/ppermute | solution.py:24
  101.2 3.5 %collective-permute-start.17 = (f32[6,6,10,1]{3,2,1,0:T(8,128)S(1)}, f32[6,6,10,1]{3,2,1,0:T(8,128)S(1)}, u32[]{:S(2)}, u32[]{:S(2)}) collective-permute-start(f32[6,6,10,1]{3,2,1,0:T(8,128)S(1)} %get-tuple-element.151), channel_id=1, source_target_pairs={{1,0},{3,2},{5,4},{7,6},{9,8},{11,10},{13,12},{15,14},{17,16},{19,... | collective-permute-start | bytes 4328 | tf_op jit(solution)/shard_map/ppermute | solution.py:26
  107.3 16.5 %collective-permute-start.20 = (f32[2,6,4,1,128]{4,3,2,1,0:T(1,128)S(1)}, f32[2,6,4,1,128]{4,3,2,1,0:T(1,128)S(1)}, u32[]{:S(2)}, u32[]{:S(2)}) collective-permute-start(f32[2,6,4,1,128]{4,3,2,1,0:T(1,128)S(1)} %get-tuple-element.155), channel_id=1, source_target_pairs={{0,2},{2,4},{4,6},{6,8},{8,10},{10,12},{12,14},{14,16},{16,18},{18... | collective-permute-start | bytes 73736 | tf_op jit(solution)/shard_map/ppermute | solution.py:24
  114.5 9.6 %collective-permute-start.21 = (f32[2,6,4,1,128]{4,3,2,1,0:T(1,128)S(1)}, f32[2,6,4,1,128]{4,3,2,1,0:T(1,128)S(1)}, u32[]{:S(2)}, u32[]{:S(2)}) collective-permute-start(f32[2,6,4,1,128]{4,3,2,1,0:T(1,128)S(1)} %get-tuple-element.156), channel_id=1, source_target_pairs={{2,0},{4,2},{6,4},{8,6},{10,8},{12,10},{14,12},{16,14},{18,16},{20... | collective-permute-start | bytes 73736 | tf_op jit(solution)/shard_map/ppermute | solution.py:26
  118.0 9.2 %collective-permute-start.19 = (f32[6,1,8,128]{3,2,1,0:T(8,128)S(1)}, f32[6,1,8,128]{3,2,1,0:T(8,128)S(1)}, u32[]{:S(2)}, u32[]{:S(2)}) collective-permute-start(f32[6,1,8,128]{3,2,1,0:T(8,128)S(1)} %get-tuple-element.171), channel_id=1, source_target_pairs={{48,0},{96,48},{144,96},{192,144},{240,192},{288,240},{336,288},{3... | collective-permute-start | bytes 73736 | tf_op jit(solution)/shard_map/ppermute | solution.py:26
  119.9 9.6 %collective-permute-start.18 = (f32[6,1,8,128]{3,2,1,0:T(8,128)S(1)}, f32[6,1,8,128]{3,2,1,0:T(8,128)S(1)}, u32[]{:S(2)}, u32[]{:S(2)}) collective-permute-start(f32[6,1,8,128]{3,2,1,0:T(8,128)S(1)} %get-tuple-element.172), channel_id=1, source_target_pairs={{0,48},{48,96},{96,144},{144,192},{192,240},{240,288},{288,336},{3... | collective-permute-start | bytes 73736 | tf_op jit(solution)/shard_map/ppermute | solution.py:24
  124.4 5.6 %collective-permute-start.22 = (f32[2,6,4,10,1]{4,3,2,1,0:T(8,128)S(1)}, f32[2,6,4,10,1]{4,3,2,1,0:T(8,128)S(1)}, u32[]{:S(2)}, u32[]{:S(2)}) collective-permute-start(f32[2,6,4,10,1]{4,3,2,1,0:T(8,128)S(1)} %get-tuple-element.144), channel_id=1, source_target_pairs={{0,1},{2,3},{4,5},{6,7},{8,9},{10,11},{12,13},{14,15},{16,17},{18,... | collective-permute-start | bytes 5768 | tf_op jit(solution)/shard_map/ppermute | solution.py:24
  125.7 4.3 %collective-permute-start.23 = (f32[2,6,4,10,1]{4,3,2,1,0:T(8,128)S(1)}, f32[2,6,4,10,1]{4,3,2,1,0:T(8,128)S(1)}, u32[]{:S(2)}, u32[]{:S(2)}) collective-permute-start(f32[2,6,4,10,1]{4,3,2,1,0:T(8,128)S(1)} %get-tuple-element.145), channel_id=1, source_target_pairs={{1,0},{3,2},{5,4},{7,6},{9,8},{11,10},{13,12},{15,14},{17,16},{19,... | collective-permute-start | bytes 5768 | tf_op jit(solution)/shard_map/ppermute | solution.py:26
where the time goes:
time: 134 us; the launch traced here: 133 us
  starting transfers between devices  82.4 us (61%)
  waiting for transfers between devices  33.9 us (25%)
  other arithmetic  11.8 us (9%)
  local copies, waits for them, and re-layouts  3.74 us (3%)
    ppermute x12, starting transfers between devices, with_halo(): lax.ppermute(tail, axis, [(i, (i + 1) % count) for i in range(ends)])  45.6 us
    ppermute x12, starting transfers between devices, with_halo(): lax.ppermute(head, axis, [((i + 1) % count, i) for i in range(ends)])  36.9 us
    ppermute x12, waiting for transfers between devices, with_halo(): lax.ppermute(head, axis, [((i + 1) % count, i) for i in range(ends)])  17.1 us
    ppermute x12, waiting for transfers between devices, with_halo(): lax.ppermute(tail, axis, [(i, (i + 1) % count) for i in range(ends)])  16.8 us
  transfers between devices with their start and end apart: 24, of which 11 were waited for; matrix products, arithmetic and copies ran while one was open for 3% of the time, Pallas kernels for 0%

commit v1 on v0

v1 whole, which is shorter than its diff:
```python
import jax
import jax.numpy as jnp
from jax import lax
from jax.experimental import pallas as pl
from jax.experimental.pallas import tpu as pltpu
from jax.sharding import PartitionSpec as P

MESH = pl.DeviceIdType.MESH
STEP_SIZE = 0.15
LIMIT_EPS = 0.03
FIX_WIDTH = 0.2
PRODUCE = 0.1355
DESTROY = 3.24

PLANES = 8
ROWS = 24

MESSAGES = (
    (1, 0, False, (4, 6), (8, 16), (0, 2), (8, 16)),
    (-1, 0, False, (2, 4), (8, 16), (6, 8), (8, 16)),
    (0, 1, False, (2, 6), (14, 16), (2, 6), (6, 8)),
    (0, -1, False, (2, 6), (8, 10), (2, 6), (16, 18)),
    (1, 1, False, (5, 6), (15, 16), (1, 2), (7, 8)),
    (1, -1, False, (5, 6), (8, 9), (1, 2), (16, 17)),
    (-1, 1, False, (2, 3), (15, 16), (6, 7), (7, 8)),
    (-1, -1, False, (2, 3), (8, 9), (6, 7), (16, 17)),
    (0, 0, True, (2, 6), (8, 16), (2, 6), (8, 16)),
    (1, 0, True, (5, 6), (8, 16), (1, 2), (8, 16)),
    (-1, 0, True, (2, 3), (8, 16), (6, 7), (8, 16)),
    (0, 1, True, (2, 6), (15, 16), (2, 6), (7, 8)),
    (0, -1, True, (2, 6), (8, 9), (2, 6), (16, 17)),
)
COUNT = len(MESSAGES)


def across(ref, m, row):
    return ref.at[pl.ds(m * PLANES * ROWS + row, 8, stride=ROWS), :]


def flat(ref):
    return ref.reshape(6 * PLANES * ROWS, 128)


def conserved(p):
    q = 0.5 * (p[1] * p[1] + p[2] * p[2] + p[3] * p[3])
    return [p[0], p[0] * p[1], p[0] * p[2], p[0] * p[3], 2.5 * p[4] + p[0] * q, p[0] * p[5]]


def primitive(u):
    inv = 1.0 / u[0]
    v = [u[1] * inv, u[2] * inv, u[3] * inv]
    pressure = 0.4 * (u[4] - 0.5 * u[0] * (v[0] * v[0] + v[1] * v[1] + v[2] * v[2]))
    return [u[0], v[0], v[1], v[2], pressure, u[5] * inv]


def limit(e, cp, cm, ap, am, rp, rm):
    dc, da, dr = cp - cm, ap - am, rp - rm
    top = jnp.maximum(jnp.maximum(jnp.maximum(cp, cm), jnp.maximum(ap, am)), jnp.maximum(jnp.maximum(rp, rm), e))
    low = jnp.minimum(jnp.minimum(jnp.minimum(cp, cm), jnp.minimum(ap, am)), jnp.minimum(jnp.minimum(rp, rm), e))
    bound = jnp.minimum(top - e, e - low)
    delta = 0.25 * jnp.maximum(jnp.maximum(jnp.abs(dc), jnp.abs(da)), jnp.abs(dr))
    square = bound * bound + LIMIT_EPS
    cross = bound * delta
    factor = jnp.minimum(1.0, (square + 2.0 * cross) / (square + cross + 2.0 * delta * delta))
    quarter = 0.25 * factor
    return (quarter * dc, quarter * da, quarter * dr), (dc, da, dr)


def fix(speed):
    size = jnp.abs(speed)
    return jnp.where(size < FIX_WIDTH, speed * speed * (0.5 / FIX_WIDTH) + 0.5 * FIX_WIDTH, size)


def side(s, d):
    y = lax.rsqrt(s[0])
    root = s[0] * y
    q = 0.5 * (s[1] * s[1] + s[2] * s[2] + s[3] * s[3])
    h = 3.5 * s[4] * (y * y) + q
    m = s[0] * s[d + 1]
    f = [m, m * s[1], m * s[2], m * s[3], m * h, m * s[5]]
    f[d + 1] = f[d + 1] + s[4]
    return root, h, f


def roe(left, right, d):
    rl, hl, fl = side(left, d)
    rr, hr, fr = side(right, d)
    jump = [r - l for l, r in zip(left, right)]
    w = rr / (rl + rr)
    vel = [left[k] + w * jump[k] for k in (1, 2, 3)]
    h = hl + w * (hr - hl)
    nu = left[5] + w * jump[5]
    un = vel[d]
    q = 0.5 * (vel[0] * vel[0] + vel[1] * vel[1] + vel[2] * vel[2])
    c2 = 0.4 * (h - q)
    ic = lax.rsqrt(c2)
    c = c2 * ic
    dens = rl * rr
    x = 0.5 * jump[4] * (ic * ic)
    y = 0.5 * dens * jump[d + 1] * ic
    mid = fix(un)
    slow = fix(un - c) * (x - y)
    fast = fix(un + c) * (x + y)
    both = slow + fast
    wave = mid * (jump[0] - 2.0 * x)
    total = both + wave
    skew = c * (fast - slow)
    shear = mid * dens
    dis = [total]
    inner = None
    for k in range(3):
        if k == d:
            dis.append(total * vel[k] + skew)
        else:
            part = shear * jump[k + 1]
            dis.append(total * vel[k] + part)
            inner = vel[k] * part if inner is None else inner + vel[k] * part
    dis.append(both * h + un * skew + wave * q + inner)
    dis.append(total * nu + shear * jump[5])
    return [fl[k] + fr[k] - dis[k] for k in range(6)]


def kernel(
    flow, inflow, walls, out,
    g1, g2, p1, p2, rs1, rs2, rr1, rr2, lc, rc, ap, am, lr, rr, src, fc, fa, fr, half, ns, entry, kinds,
    local_sem, send_sem, recv_sem, rad_send, rad_recv,
):
    ci, ai, ri = lax.axis_index("circ"), lax.axis_index("axial"), lax.axis_index("rad")
    nc, na = lax.axis_size("circ"), lax.axis_size("axial")
    other = 1 - ri
    first, last = ai == 0, ai == na - 1

    def target(dc, da, cross):
        return {"circ": lax.rem(ci + dc + nc, nc), "axial": ai + da, "rad": other if cross else ri}

    def there(da):
        return ai < na - 1 if da > 0 else ai > 0

    def guard(da, act):
        if da == 0:
            act()
        else:
            pl.when(there(da))(act)

    barrier = pltpu.get_barrier_semaphore()
    for dc, da, cross, *_ in MESSAGES:
        guard(da, lambda dc=dc, da=da, cross=cross: pl.semaphore_signal(
            barrier, inc=1, device_id=target(dc, da, cross), device_id_type=MESH))

    load = pltpu.make_async_copy(flow, g1.at[:, 2:6, 8:16, :], local_sem.at[0])
    load.start()
    lanes_from = pl.multiple_of(ri * 128, 128)
    enter = pltpu.make_async_copy(inflow.at[:, :, pl.ds(lanes_from, 128)], entry, local_sem.at[1])
    enter.start()
    kind = pltpu.make_async_copy(walls, kinds, local_sem.at[2])
    kind.start()
    load.wait()
    enter.wait()
    kind.wait()

    def message(phase, k):
        dc, da, cross, sp, sr, tp, tr = MESSAGES[k]
        own = (g1, g2)[phase]
        into = (p1, p2)[phase] if cross else own
        return pltpu.make_async_remote_copy(
            src_ref=own.at[:, sp[0]:sp[1], sr[0]:sr[1], :],
            dst_ref=into.at[:, tp[0]:tp[1], tr[0]:tr[1], :],
            send_sem=send_sem.at[phase, k],
            recv_sem=recv_sem.at[phase, k],
            device_id=target(dc, da, cross),
            device_id_type=MESH,
        )

    def send(phase):
        for k in range(COUNT):
            guard(MESSAGES[k][1], lambda k=k: message(phase, k).start())

    def receive(phase):
        for k in range(COUNT):
            guard(-MESSAGES[k][1], lambda k=k: message(phase, k).wait_recv())

    def sent(phase):
        for k in range(COUNT):
            guard(MESSAGES[k][1], lambda k=k: message(phase, k).wait_send())

    lane = lax.broadcasted_iota(jnp.int32, (8, 128), 1)
    at_first, at_last = lane == 0, lane == 127
    half_lane = jnp.where(lane >= 64, 1, 0)
    wall_lane = half_lane == 1 - ri
    wall_turn = jnp.where(ri == 0, 127, 1)
    radial = ri * 128 + lane
    wall_inv = 1.0 / (jnp.minimum(radial, 255 - radial) + 1).astype(jnp.float32)

    def ghost(e, beside, sign):
        return jnp.where(wall_lane, pltpu.roll(e * sign, wall_turn, 1), beside)

    def around(e, g):
        return pltpu.roll(jnp.where(at_first, g, e), 127, 1), pltpu.roll(jnp.where(at_last, g, e), 1, 1)

    for row in range(7, 17):
        station = jnp.clip(ai * 8 + (row - 8), 0, na * 8 - 1)
        value = jnp.where(kinds[ri, station] == 1, -1.0, 1.0)
        ns[pl.ds(row, 1), :] = jnp.full((1, 128), value, jnp.float32)

    def signs(tile):
        return (1.0, tile, tile, -1.0, 1.0, tile)

    def ends(own):
        @pl.when(first)
        def _():
            for m in range(6):
                for plane in range(1, 7):
                    at = lax.rem(ci * 4 + (plane - 2) + nc * 4, nc * 4)
                    own[m, plane, 7:8, :] = entry[m, pl.ds(at, 1), :]

        @pl.when(last)
        def _():
            for m in range(6):
                for plane in range(1, 7):
                    own[m, plane, 16:17, :] = own[m, plane, 15:16, :]

    def slopes(phase):
        own, beside = (g1, g2)[phase], (p1, p2)[phase]
        rs = (rs1, rs2)[phase]
        tile_sign = signs(ns[8:16, :])
        outward = jnp.where(ri == 0, 1.0, -1.0)

        def plane_step(c, carry):
            velocity = []
            for m in range(6):
                e = own[m, c, 8:16, :]
                g = ghost(e, beside[m, c, 8:16, :], tile_sign[m])
                rp, rm = around(e, g)
                hs, diff = limit(
                    e, own[m, c + 1, 8:16, :], own[m, c - 1, 8:16, :], own[m, c, 9:17, :], own[m, c, 7:15, :], rp, rm
                )
                velocity.append(diff)
                lc[m, c] = e + hs[0]
                rc[m, c] = e - hs[0]
                ap[m, c, 8:16, :] = e + hs[1]
                am[m, c, 8:16, :] = e - hs[1]
                lr[m, c] = e + hs[2]
                rr[m, c] = e - hs[2]
                rs[m, c] = e + outward * hs[2]
            oc = velocity[3][1] - velocity[2][2]
            oa = velocity[1][2] - velocity[3][0]
            orr = velocity[2][0] - velocity[1][1]
            s = jnp.sqrt(oc * oc + oa * oa + orr * orr)
            dens, nu = own[0, c, 8:16, :], own[5, c, 8:16, :]
            ratio = nu * wall_inv
            src[c] = (0.5 * PRODUCE) * s * dens * nu - DESTROY * dens * (ratio * ratio)
            return carry

        lax.fori_loop(1, 7, plane_step, 0)

        own_f, beside_f, ap_f, am_f = flat(own), flat(beside), flat(ap), flat(am)
        for row, held, step in ((7, first, 1.0), (16, last, -1.0)):
            row_sign = signs(jnp.broadcast_to(ns[row:row + 1, :], (8, 128)))
            for m in range(6):
                e = across(own_f, m, row)[...]
                g = ghost(e, across(beside_f, m, row)[...], row_sign[m])
                rp, rm = around(e, g)
                hs, _ = limit(
                    e, pltpu.roll(e, 7, 0), pltpu.roll(e, 1, 0), across(own_f, m, row + 1)[...],
                    across(own_f, m, row - 1)[...], rp, rm
                )
                into = across(ap_f if step > 0 else am_f, m, row)
                into[...] = e + jnp.where(held, 0.0, step * hs[1])

    def swap(phase):
        rs, rr_in = (rs1, rs2)[phase], (rr1, rr2)[phase]
        return pltpu.make_async_remote_copy(
            src_ref=rs.at[:, 2:6], dst_ref=rr_in, send_sem=rad_send.at[phase], recv_sem=rad_recv.at[phase],
            device_id={"circ": ci, "axial": ai, "rad": other}, device_id_type=MESH,
        )

    def faces():
        def circ_step(c, carry):
            f = roe([lc[m, c - 1] for m in range(6)], [rc[m, c] for m in range(6)], 0)
            for m in range(6):
                fc[m, c] = f[m]
            return carry

        lax.fori_loop(2, 7, circ_step, 0)

        def axial_step(c, carry):
            f = roe([ap[m, c, 7:15, :] for m in range(6)], [am[m, c, 8:16, :] for m in range(6)], 1)
            for m in range(6):
                fa[m, c, 8:16, :] = f[m]
            return carry

        lax.fori_loop(2, 6, axial_step, 0)
        ap_f, am_f, fa_f = flat(ap), flat(am), flat(fa)
        f = roe([across(ap_f, m, 15)[...] for m in range(6)], [across(am_f, m, 16)[...] for m in range(6)], 1)
        for m in range(6):
            across(fa_f, m, 16)[...] = f[m]

    def finish(phase):
        own, rr_in = (g1, g2)[phase], (rr1, rr2)[phase]
        tile_sign = signs(ns[8:16, :])
        pack_l = [jnp.full((8, 128), v, jnp.float32) for v in (1.0, 0.0, 0.0, 0.0, 1.0, 0.0)]
        pack_r = list(pack_l)
        for c in range(4):
            for m in range(6):
                g = ghost(own[m, c + 2, 8:16, :], rr_in[m, c], tile_sign[m])
                fr[m, c] = g
                pack_l[m] = jnp.where(lane == c, pltpu.roll(lr[m, c + 2], c + 1, 1), pack_l[m])
                pack_r[m] = jnp.where(lane == c, pltpu.roll(g, c, 1) if c else g, pack_r[m])
        extra = roe(pack_l, pack_r, 2)

        def step(c, carry):
            left = [pltpu.roll(jnp.where(at_last, fr[m, c], lr[m, c + 2]), 1, 1) for m in range(6)]
            f = roe(left, [rr[m, c + 2] for m in range(6)], 2)
            u0 = conserved([own[m, c + 2, 8:16, :] for m in range(6)])
            change = []
            for m in range(6):
                after = jnp.where(at_last, pltpu.roll(extra[m], 127 - c, 1), pltpu.roll(f[m], 127, 1))
                total = (
                    (fc[m, c + 3] - fc[m, c + 2])
                    + (fa[m, c + 2, 9:17, :] - fa[m, c + 2, 8:16, :])
                    + (after - f[m])
                )
                change.append((-0.5 * STEP_SIZE) * total)
            change[5] = change[5] + STEP_SIZE * src[c + 2]
            if phase == 0:
                u1 = [u0[m] + change[m] for m in range(6)]
                w = primitive(u1)
                for m in range(6):
                    g2[m, c + 2, 8:16, :] = w[m]
                    half[m, c] = 0.5 * (u0[m] + u1[m])
            else:
                for m in range(6):
                    out[m, c] = half[m, c] + 0.5 * change[m]
            return carry

        lax.fori_loop(0, 4, step, 0)

    pl.semaphore_wait(barrier, COUNT - 4 * first.astype(jnp.int32) - 4 * last.astype(jnp.int32))
    for phase in range(2):
        send(phase)
        receive(phase)
        ends((g1, g2)[phase])
        slopes(phase)
        swap(phase).start()
        faces()
        swap(phase).wait_recv()
        finish(phase)
    for phase in range(2):
        sent(phase)
        swap(phase).wait_send()


def solution(mesh):
    def vmem(*shape):
        return pltpu.VMEM(shape, jnp.float32)

    def body(flow, inflow, wall_kind):
        padded = (6, PLANES, ROWS, 128)
        tiles = (6, PLANES, 8, 128)
        inner = (6, 4, 8, 128)
        return pl.pallas_call(
            kernel,
            out_shape=jax.ShapeDtypeStruct(flow.shape, jnp.float32),
            in_specs=[pl.BlockSpec(memory_space=pl.ANY)] * 3,
            out_specs=pl.BlockSpec(memory_space=pltpu.VMEM),
            scratch_shapes=[
                vmem(*padded), vmem(*padded), vmem(*padded), vmem(*padded),
                vmem(*tiles), vmem(*tiles), vmem(*inner), vmem(*inner),
                vmem(*tiles), vmem(*tiles), vmem(*padded), vmem(*padded), vmem(*tiles), vmem(*tiles),
                vmem(PLANES, 8, 128), vmem(*tiles), vmem(*padded), vmem(*inner), vmem(*inner),
                vmem(ROWS, 128), vmem(6, inflow.shape[1], 128),
                pltpu.SMEM((2, wall_kind.shape[0]), jnp.int32),
                pltpu.SemaphoreType.DMA((3,)),
                pltpu.SemaphoreType.DMA((2, COUNT)), pltpu.SemaphoreType.DMA((2, COUNT)),
                pltpu.SemaphoreType.DMA((2,)), pltpu.SemaphoreType.DMA((2,)),
            ],
            compiler_params=pltpu.CompilerParams(
                collective_id=0, has_side_effects=True, vmem_limit_bytes=56 * 2**20
            ),
        )(flow, inflow, wall_kind.T)

    spec = P(None, "circ", "axial", "rad")
    return jax.shard_map(body, mesh=mesh, in_specs=(spec, P(), P()), out_specs=spec, check_vma=False)
```

time: 134 us -> 35.6 us (0.27)
  the two profiles are of different devices: /device:TPU:192 before, /device:TPU:1 now
where the time goes in v1:
time: 35.6 us; the launch traced here: 35.4 us
  Pallas kernels  33.8 us (95%)
  local copies, waits for them, and re-layouts  1.54 us (4%)
    pallas_call x1, Pallas kernels, body(): pl.pallas_call(kernel, out_shape=jax.ShapeDtypeStruct(flow.shape, jnp.flo...  33.8 us
    unnamed x1, local copies, waits for them, and re-layouts  1.54 us

profile of v1, /device:TPU:1, one launch (start us, length us, event | category | flops | bytes accessed | tf_op | source)
XLA Modules:
  0.0 35.4 jit_solution(8432121640907591049)
XLA Ops:
  0.0 33.8 %shard_map.37 = f32[6,4,8,128]{3,2,1,0:T(8,128)} custom-call(f32[6,4,8,128]{3,2,1,0:T(8,128)} %flow.1, f32[6,64,256]{2,1,0:T(8,128)} %inflow.1, s32[2,192]{1,0:T(2,128)} %bitcast.1), custom_call_target="tpu_custom_call" | custom-call | tf_op jit(solution)/shard_map/pallas_call | solution.py:361
  33.8 1.5 %copy.5 = f32[6,4,8,128]{3,2,1,0:T(8,128)} copy(f32[6,4,8,128]{3,2,1,0:T(8,128)} %shard_map.37) | data formatting | bytes 196608

commit v2 on v1

v2 whole, which is shorter than its diff:
```python
import jax
import jax.numpy as jnp
from jax import lax
from jax.experimental import pallas as pl
from jax.experimental.pallas import tpu as pltpu
from jax.sharding import PartitionSpec as P

MESH = pl.DeviceIdType.MESH
STEP_SIZE = 0.15
LIMIT_EPS = 0.03
FIX_WIDTH = 0.2
PRODUCE = 0.1355
DESTROY = 3.24

PLANES = 8
ROWS = 24

MESSAGES = (
    (0, 1, (2, 6), (14, 16), (2, 6), (6, 8)),
    (0, -1, (2, 6), (8, 10), (2, 6), (16, 18)),
    (1, 1, (5, 6), (15, 16), (1, 2), (7, 8)),
    (1, -1, (5, 6), (8, 9), (1, 2), (16, 17)),
    (-1, 1, (2, 3), (15, 16), (6, 7), (7, 8)),
    (-1, -1, (2, 3), (8, 9), (6, 7), (16, 17)),
    (1, 0, (4, 6), (8, 16), (0, 2), (8, 16)),
    (-1, 0, (2, 4), (8, 16), (6, 8), (8, 16)),
)
PACKED = (
    (0, 1, (0, 16)),
    (0, -1, (8, 24)),
    (1, 0, (8, 16)),
    (-1, 0, (8, 16)),
    (0, 0, (8, 16)),
)
FAR, BESIDE = len(MESSAGES), len(PACKED)


def slot(m, c):
    return 2 * (m * 6 + 1 + c)


def across(ref, phase, m, row, first=0, count=8):
    return ref.at[pl.ds(((phase * 6 + m) * PLANES + first) * ROWS + row, count, stride=ROWS), :]


def flat(ref):
    return ref.reshape(ref.size // 128, 128)


def conserved(p):
    q = 0.5 * (p[1] * p[1] + p[2] * p[2] + p[3] * p[3])
    return [p[0], p[0] * p[1], p[0] * p[2], p[0] * p[3], 2.5 * p[4] + p[0] * q, p[0] * p[5]]


def primitive(u):
    inv = 1.0 / u[0]
    v = [u[1] * inv, u[2] * inv, u[3] * inv]
    pressure = 0.4 * (u[4] - 0.5 * u[0] * (v[0] * v[0] + v[1] * v[1] + v[2] * v[2]))
    return [u[0], v[0], v[1], v[2], pressure, u[5] * inv]


def limit(e, cp, cm, ap, am, rp, rm):
    dc, da, dr = cp - cm, ap - am, rp - rm
    top = jnp.maximum(jnp.maximum(jnp.maximum(cp, cm), jnp.maximum(ap, am)), jnp.maximum(jnp.maximum(rp, rm), e))
    low = jnp.minimum(jnp.minimum(jnp.minimum(cp, cm), jnp.minimum(ap, am)), jnp.minimum(jnp.minimum(rp, rm), e))
    bound = jnp.minimum(top - e, e - low)
    delta = 0.25 * jnp.maximum(jnp.maximum(jnp.abs(dc), jnp.abs(da)), jnp.abs(dr))
    square = bound * bound + LIMIT_EPS
    cross = bound * delta
    factor = jnp.minimum(1.0, (square + 2.0 * cross) / (square + cross + 2.0 * delta * delta))
    quarter = 0.25 * factor
    return (quarter * dc, quarter * da, quarter * dr), (dc, da, dr)


def fix(speed):
    size = jnp.abs(speed)
    return jnp.where(size < FIX_WIDTH, speed * speed * (0.5 / FIX_WIDTH) + 0.5 * FIX_WIDTH, size)


def side(s, d):
    y = lax.rsqrt(s[0])
    root = s[0] * y
    q = 0.5 * (s[1] * s[1] + s[2] * s[2] + s[3] * s[3])
    h = 3.5 * s[4] * (y * y) + q
    m = s[0] * s[d + 1]
    f = [m, m * s[1], m * s[2], m * s[3], m * h, m * s[5]]
    f[d + 1] = f[d + 1] + s[4]
    return root, h, f


def roe(left, right, d):
    rl, hl, fl = side(left, d)
    rr, hr, fr = side(right, d)
    jump = [r - l for l, r in zip(left, right)]
    w = rr / (rl + rr)
    vel = [left[k] + w * jump[k] for k in (1, 2, 3)]
    h = hl + w * (hr - hl)
    nu = left[5] + w * jump[5]
    un = vel[d]
    q = 0.5 * (vel[0] * vel[0] + vel[1] * vel[1] + vel[2] * vel[2])
    c2 = 0.4 * (h - q)
    ic = lax.rsqrt(c2)
    c = c2 * ic
    dens = rl * rr
    x = 0.5 * jump[4] * (ic * ic)
    y = 0.5 * dens * jump[d + 1] * ic
    mid = fix(un)
    slow = fix(un - c) * (x - y)
    fast = fix(un + c) * (x + y)
    both = slow + fast
    wave = mid * (jump[0] - 2.0 * x)
    total = both + wave
    skew = c * (fast - slow)
    shear = mid * dens
    dis = [total]
    inner = None
    for k in range(3):
        if k == d:
            dis.append(total * vel[k] + skew)
        else:
            part = shear * jump[k + 1]
            dis.append(total * vel[k] + part)
            inner = vel[k] * part if inner is None else inner + vel[k] * part
    dis.append(both * h + un * skew + wave * q + inner)
    dis.append(total * nu + shear * jump[5])
    return [fl[k] + fr[k] - dis[k] for k in range(6)]


def kernel(
    flow, inflow, walls, out,
    g, pack, land, packed, edge, lc, rc, ap, am, lr, rr, src, fa, ns, entry, entry_packed, kinds,
    local_sem, send_sem, recv_sem,
):
    ci, ai, ri = lax.axis_index("circ"), lax.axis_index("axial"), lax.axis_index("rad")
    nc, na = lax.axis_size("circ"), lax.axis_size("axial")
    first, last = ai == 0, ai == na - 1

    def target(dc, da, cross):
        return {"circ": lax.rem(ci + dc + nc, nc), "axial": ai + da, "rad": 1 - ri if cross else ri}

    def there(da):
        return ai < na - 1 if da > 0 else ai > 0

    def guard(da, act):
        if da == 0:
            act()
        else:
            pl.when(there(da))(act)

    barrier = pltpu.get_barrier_semaphore()
    for cross, group in ((False, MESSAGES), (True, PACKED)):
        for dc, da, *_ in group:
            guard(da, lambda dc=dc, da=da, cross=cross: pl.semaphore_signal(
                barrier, inc=1, device_id=target(dc, da, cross), device_id_type=MESH))

    load = pltpu.make_async_copy(flow, g.at[0, :, 2:6, 8:16, :], local_sem.at[0])
    load.start()
    kind = pltpu.make_async_copy(walls, kinds, local_sem.at[1])
    kind.start()
    enter = [
        pltpu.make_async_copy(
            inflow.at[:, :, pl.ds(pl.multiple_of(core * 128, 128), 128)], entry.at[k], local_sem.at[2 + k])
        for k, core in enumerate((ri, 1 - ri))
    ]
    for part in enter:
        part.start()

    def far(phase, k):
        dc, da, sp, sr, tp, tr = MESSAGES[k]
        return pltpu.make_async_remote_copy(
            src_ref=g.at[phase, :, sp[0]:sp[1], sr[0]:sr[1], :],
            dst_ref=g.at[phase, :, tp[0]:tp[1], tr[0]:tr[1], :],
            send_sem=send_sem.at[phase, k],
            recv_sem=recv_sem.at[phase, k],
            device_id=target(dc, da, False),
            device_id_type=MESH,
        )

    def beside(phase, k):
        dc, da, rows = PACKED[k]
        return pltpu.make_async_remote_copy(
            src_ref=pack.at[phase, rows[0]:rows[1], :],
            dst_ref=land.at[phase, k, rows[0]:rows[1], :],
            send_sem=send_sem.at[phase, FAR + k],
            recv_sem=recv_sem.at[phase, FAR + k],
            device_id=target(dc, da, True),
            device_id_type=MESH,
        )

    def each(group, act, back, wanted):
        for k, (dc, da, *_) in enumerate(group):
            if (da != 0) in wanted:
                guard(-da if back else da, lambda k=k: act(k))

    lane = lax.broadcasted_iota(jnp.int32, (8, 128), 1)
    at_first, at_last = lane == 0, lane == 127
    hub_lane, casing_lane = lane + 128 * ri == 0, lane + 128 * ri == 255
    radial = ri * 128 + lane
    wall_inv = 1.0 / (jnp.minimum(radial, 255 - radial) + 1).astype(jnp.float32)
    inner_turn = jnp.where(ri == 0, 127, 1)

    def around(e, near, sign):
        mirror = e * sign
        after = pltpu.roll(jnp.where(at_first, near, e), 127, 1)
        before = pltpu.roll(jnp.where(at_last, near, e), 1, 1)
        return jnp.where(casing_lane, mirror, after), jnp.where(hub_lane, mirror, before)

    def signs(tile):
        return (1.0, tile, tile, -1.0, 1.0, tile)

    def fill(phase):
        tile = jnp.zeros((8, 128), jnp.float32)
        for m in range(6):
            for c in range(4):
                at = slot(m, c)
                e = g[phase, m, c + 2, 8:16, :]
                turned = pltpu.roll(e, jnp.where(ri == 0, (at + 2) % 128, at), 1)
                tile = jnp.where((lane == at) | (lane == at + 1), turned, tile)
        pack[phase, 8:16, :] = tile
        for row, start in ((15, 0), (8, 16)):
            tile = jnp.zeros((4, 128), jnp.float32)
            for m in range(6):
                e = across(flat(g), phase, m, row, 2, 4)[...]
                here = lane[0:4] == lax.rem(m + 127 * (1 - ri), 128)
                tile = jnp.where(here, pltpu.roll(e, m, 1) if m else e, tile)
            pack[phase, start:start + 4, :] = tile

    def station_signs():
        for row in range(7, 17):
            station = jnp.clip(ai * 8 + (row - 8), 0, na * 8 - 1)
            value = jnp.where(kinds[ri, station] == 1, -1.0, 1.0)
            ns[pl.ds(row, 1), :] = jnp.full((1, 128), value, jnp.float32)

    def entry_rows():
        row = jnp.zeros((1, 128), jnp.float32)
        for m in range(6):
            for plane in range(1, 7):
                at = lax.rem(ci * 4 + (plane - 2) + nc * 4, nc * 4)
                mine = entry[0, m, pl.ds(at, 1), :]
                for phase in range(2):
                    g[phase, m, plane, 7:8, :] = mine
                if 2 <= plane < 6:
                    theirs = entry[1, m, pl.ds(at, 1), :]
                    k = slot(m, plane - 2)
                    turned = pltpu.roll(
                        jnp.broadcast_to(theirs, (8, 128)), jnp.where(ri == 0, k, (k + 2) % 128), 1)[0:1]
                    row = jnp.where((lane[0:1] == k) | (lane[0:1] == k + 1), turned, row)
        entry_packed[0:1, :] = row

    def section(phase, carry):
        each(MESSAGES, lambda k: far(phase, k).start(), False, (True,))
        each(PACKED, lambda k: beside(phase, k).start(), False, (True, False))
        each(MESSAGES, lambda k: far(phase, k).start(), False, (False,))
        each(PACKED, lambda k: beside(phase, k).wait_recv(), True, (False,))
        each(MESSAGES, lambda k: far(phase, k).wait_recv(), True, (False,))

        place = lax.rem(lane // 2, 6)
        halo = jnp.where(place == 0, pltpu.roll(land[phase, 2, 8:16, :], 120, 1), land[phase, 4, 8:16, :])
        halo = jnp.where(place == 5, pltpu.roll(land[phase, 3, 8:16, :], 8, 1), halo)
        packed[8:16, :] = halo
        turned = pltpu.roll(halo, jnp.where(ri == 0, 0, 126), 1)
        for c in range(-1, 5):
            for m in range(6):
                edge[m, c + 2] = pltpu.roll(turned, (128 - slot(m, c)) % 128, 1)

        each(PACKED, lambda k: beside(phase, k).wait_recv(), True, (True,))
        each(MESSAGES, lambda k: far(phase, k).wait_recv(), True, (True,))

        @pl.when(first)
        def _():
            packed[7:8, :] = entry_packed[0:1, :]

        @pl.when(jnp.logical_not(first))
        def _():
            packed[7:8, :] = land[phase, 0, 15:16, :]

        @pl.when(last)
        def _():
            packed[16:17, :] = packed[15:16, :]
            for m in range(6):
                for plane in range(1, 7):
                    g[phase, m, plane, 16:17, :] = g[phase, m, plane, 15:16, :]

        @pl.when(jnp.logical_not(last))
        def _():
            packed[16:17, :] = land[phase, 1, 8:9, :]

        z = packed[8:16, :]
        beyond, mine = pltpu.roll(z, inner_turn, 1), pltpu.roll(pack[phase, 8:16, :], inner_turn, 1)
        hs, _ = limit(
            z, pltpu.roll(z, 126, 1), pltpu.roll(z, 2, 1), packed[9:17, :], packed[7:15, :], beyond, mine
        )
        near_face = pltpu.roll(z - hs[2], jnp.where(ri == 0, 0, 126), 1)

        tile_sign = signs(ns[8:16, :])
        for c in range(1, 7):
            diffs = []
            for m in range(6):
                e = g[phase, m, c, 8:16, :]
                rp, rm = around(e, edge[m, c], tile_sign[m])
                hs, diff = limit(
                    e, g[phase, m, c + 1, 8:16, :], g[phase, m, c - 1, 8:16, :],
                    g[phase, m, c, 9:17, :], g[phase, m, c, 7:15, :], rp, rm
                )
                diffs.append(diff)
                lc[m, c] = e + hs[0]
                rc[m, c] = e - hs[0]
                if 2 <= c < 6:
                    ap[m, c, 8:16, :] = e + hs[1]
                    am[m, c, 8:16, :] = e - hs[1]
                    lr[m, c - 2] = e + hs[2]
                    rr[m, c - 2] = e - hs[2]
            if 2 <= c < 6:
                oc = diffs[3][1] - diffs[2][2]
                oa = diffs[1][2] - diffs[3][0]
                orr = diffs[2][0] - diffs[1][1]
                s = jnp.sqrt(oc * oc + oa * oa + orr * orr)
                dens, nu = g[phase, 0, c, 8:16, :], g[phase, 5, c, 8:16, :]
                ratio = nu * wall_inv
                src[c - 2] = (0.5 * PRODUCE) * s * dens * nu - DESTROY * dens * (ratio * ratio)

        g_f, ap_f, am_f, fa_f = flat(g), flat(ap), flat(am), flat(fa)
        for k, row, held, step in ((0, 7, first, 1.0), (1, 16, last, -1.0)):
            row_sign = signs(jnp.broadcast_to(ns[row:row + 1, :], (8, 128)))
            columns = pltpu.roll(land[phase, k, (0, 16)[k]:(8, 24)[k], :], 2, 0)
            for m in range(6):
                e = across(g_f, phase, m, row)[...]
                rp, rm = around(e, pltpu.roll(columns, 128 - m, 1) if m else columns, row_sign[m])
                hs, _ = limit(
                    e, pltpu.roll(e, 7, 0), pltpu.roll(e, 1, 0), across(g_f, phase, m, row + 1)[...],
                    across(g_f, phase, m, row - 1)[...], rp, rm
                )
                across(ap_f if step > 0 else am_f, 0, m, row)[...] = e + jnp.where(held, 0.0, step * hs[1])

        for c in range(2, 6):
            f = roe([ap[m, c, 7:15, :] for m in range(6)], [am[m, c, 8:16, :] for m in range(6)], 1)
            for m in range(6):
                fa[m, c, 8:16, :] = f[m]
        f = roe([across(ap_f, 0, m, 15)[...] for m in range(6)], [across(am_f, 0, m, 16)[...] for m in range(6)], 1)
        for m in range(6):
            across(fa_f, 0, m, 16)[...] = f[m]

        pack_l = [jnp.full((8, 128), v, jnp.float32) for v in (1.0, 0.0, 0.0, 0.0, 1.0, 0.0)]
        pack_r = list(pack_l)
        nears = []
        for c in range(4):
            nears.append([])
            for m in range(6):
                near = pltpu.roll(near_face, (128 - slot(m, c)) % 128, 1)
                nears[c].append(near)
                e = g[phase, m, c + 2, 8:16, :] * tile_sign[m]
                wall = pltpu.roll(e, c + 1, 1)
                pack_l[m] = jnp.where(lane == c, pltpu.roll(lr[m, c], c + 1, 1), pack_l[m])
                after = jnp.where(ri == 0, pltpu.roll(near, c, 1) if c else near, wall)
                pack_r[m] = jnp.where(lane == c, after, pack_r[m])
        extra = roe(pack_l, pack_r, 2)

        fc = roe([lc[m, 1] for m in range(6)], [rc[m, 2] for m in range(6)], 0)
        for c in range(4):
            fc_next = roe([lc[m, c + 2] for m in range(6)], [rc[m, c + 3] for m in range(6)], 0)
            e = [g[phase, m, c + 2, 8:16, :] for m in range(6)]
            left = [
                jnp.where(
                    hub_lane, e[m] * tile_sign[m], pltpu.roll(jnp.where(at_last, nears[c][m], lr[m, c]), 1, 1)
                )
                for m in range(6)
            ]
            fr = roe(left, [rr[m, c] for m in range(6)], 2)
            u0 = conserved(e)
            u1 = []
            for m in range(6):
                after = jnp.where(at_last, pltpu.roll(extra[m], 127 - c, 1), pltpu.roll(fr[m], 127, 1))
                total = (
                    (fc_next[m] - fc[m])
                    + (fa[m, c + 2, 9:17, :] - fa[m, c + 2, 8:16, :])
                    + (after - fr[m])
                )
                change = (-0.5 * STEP_SIZE) * total
                if m == 5:
                    change = change + STEP_SIZE * src[c]
                u1.append(u0[m] + change)
                out[m, c] = jnp.where(phase == 0, u0[m], out[m, c]) + 0.5 * change
            w = primitive(u1)
            for m in range(6):
                g[phase + 1, m, c + 2, 8:16, :] = w[m]
            fc = fc_next
        fill(phase + 1)
        return carry

    load.wait()
    kind.wait()
    for part in enter:
        part.wait()
    station_signs()
    pl.when(first)(entry_rows)
    fill(0)
    pl.semaphore_wait(barrier, FAR + BESIDE - 4 * first.astype(jnp.int32) - 4 * last.astype(jnp.int32))
    lax.fori_loop(0, 2, section, 0)
    for phase in range(2):
        each(MESSAGES, lambda k: far(phase, k).wait_send(), False, (True, False))
        each(PACKED, lambda k: beside(phase, k).wait_send(), False, (True, False))


def solution(mesh):
    def vmem(*shape):
        return pltpu.VMEM(shape, jnp.float32)

    def body(flow, inflow, wall_kind):
        padded = (6, PLANES, ROWS, 128)
        tiles = (6, PLANES, 8, 128)
        inner = (6, 4, 8, 128)
        return pl.pallas_call(
            kernel,
            out_shape=jax.ShapeDtypeStruct(flow.shape, jnp.float32),
            in_specs=[pl.BlockSpec(memory_space=pl.ANY)] * 3,
            out_specs=pl.BlockSpec(memory_space=pltpu.VMEM),
            scratch_shapes=[
                vmem(3, *padded), vmem(3, 24, 128), vmem(2, BESIDE, 24, 128), vmem(24, 128),
                vmem(*tiles), vmem(*tiles), vmem(*tiles), vmem(*padded), vmem(*padded), vmem(*inner), vmem(*inner),
                vmem(4, 8, 128), vmem(*padded), vmem(ROWS, 128), vmem(2, 6, inflow.shape[1], 128), vmem(8, 128),
                pltpu.SMEM((2, wall_kind.shape[0]), jnp.int32),
                pltpu.SemaphoreType.DMA((4,)),
                pltpu.SemaphoreType.DMA((2, FAR + BESIDE)), pltpu.SemaphoreType.DMA((2, FAR + BESIDE)),
            ],
            compiler_params=pltpu.CompilerParams(
                collective_id=0, has_side_effects=True, vmem_limit_bytes=56 * 2**20
            ),
        )(flow, inflow, wall_kind.T)

    spec = P(None, "circ", "axial", "rad")
    return jax.shard_map(body, mesh=mesh, in_specs=(spec, P(), P()), out_specs=spec, check_vma=False)
```

time: 35.6 us -> 31.1 us (0.87)
  Pallas kernels: 33.8 us -> 29.4 us
    pallas_call x1, Pallas kernels: 33.8 us -> 29.4 us  [body(): pl.pallas_call(kernel, out_shape=jax.ShapeDtypeStruct(flow.shape, jnp.flo...]
where the time goes in v2:
time: 31.1 us; the launch traced here: 30.9 us
  Pallas kernels  29.4 us (95%)
  local copies, waits for them, and re-layouts  1.54 us (5%)
    pallas_call x1, Pallas kernels, body(): pl.pallas_call(kernel, out_shape=jax.ShapeDtypeStruct(flow.shape, jnp.flo...  29.4 us
    unnamed x1, local copies, waits for them, and re-layouts  1.54 us

profile of v2, /device:TPU:1, one launch (start us, length us, event | category | flops | bytes accessed | tf_op | source)
XLA Modules:
  0.0 30.9 jit_solution(15095469687762779210)
XLA Ops:
  0.0 29.4 %shard_map.37 = f32[6,4,8,128]{3,2,1,0:T(8,128)} custom-call(f32[6,4,8,128]{3,2,1,0:T(8,128)} %flow.1, f32[6,64,256]{2,1,0:T(8,128)} %inflow.1, s32[2,192]{1,0:T(2,128)} %bitcast.1), custom_call_target="tpu_custom_call" | custom-call | tf_op jit(solution)/shard_map/pallas_call | solution.py:412
  29.4 1.5 %copy.5 = f32[6,4,8,128]{3,2,1,0:T(8,128)} copy(f32[6,4,8,128]{3,2,1,0:T(8,128)} %shard_map.37) | data formatting | bytes 196608

commit v3 on v2

--- a/solution.py
+++ b/solution.py
@@ -411,7 +411,7 @@
         inner = (6, 4, 8, 128)
         return pl.pallas_call(
             kernel,
-            out_shape=jax.ShapeDtypeStruct(flow.shape, jnp.float32),
+            out_shape=pltpu.VMEM(flow.shape, jnp.float32),
             in_specs=[pl.BlockSpec(memory_space=pl.ANY)] * 3,
             out_specs=pl.BlockSpec(memory_space=pltpu.VMEM),
             scratch_shapes=[

time: 31.1 us -> 29.6 us (0.952)
  local copies, waits for them, and re-layouts: 1.54 us -> 0.64 us
  Pallas kernels: 29.4 us -> 28.8 us
    unnamed x1, local copies, waits for them, and re-layouts: 1.54 us -> 0.64 us
    pallas_call x1, Pallas kernels: 29.4 us -> 28.8 us  [body(): pl.pallas_call(kernel, out_shape=pltpu.VMEM(flow.shape, jnp.float32), in_...]
where the time goes in v3:
time: 29.6 us; the launch traced here: 29.4 us
  Pallas kernels  28.8 us (97%)
  local copies, waits for them, and re-layouts  0.64 us (2%)
    pallas_call x1, Pallas kernels, body(): pl.pallas_call(kernel, out_shape=pltpu.VMEM(flow.shape, jnp.float32), in_...  28.8 us
    unnamed x1, local copies, waits for them, and re-layouts  0.64 us

profile of v3, /device:TPU:1, one launch (start us, length us, event | category | flops | bytes accessed | tf_op | source)
XLA Modules:
  0.0 29.4 jit_solution(16604207480219553439)
XLA Ops:
  0.0 28.8 %shard_map.37 = f32[6,4,8,128]{3,2,1,0:T(8,128)S(1)} custom-call(f32[6,4,8,128]{3,2,1,0:T(8,128)} %flow.1, f32[6,64,256]{2,1,0:T(8,128)} %inflow.1, s32[2,192]{1,0:T(2,128)} %bitcast.1), custom_call_target="tpu_custom_call" | custom-call | tf_op jit(solution)/shard_map/pallas_call | solution.py:412
  28.8 0.6 %copy.5 = f32[6,4,8,128]{3,2,1,0:T(8,128)} copy(f32[6,4,8,128]{3,2,1,0:T(8,128)S(1)} %shard_map.37) | data formatting | bytes 196608

commit v4 on v3

v4 whole, which is shorter than its diff:
```python
import jax
import jax.numpy as jnp
from jax import lax
from jax.experimental import pallas as pl
from jax.experimental.pallas import tpu as pltpu
from jax.sharding import PartitionSpec as P

MESH = pl.DeviceIdType.MESH
STEP_SIZE = 0.15
LIMIT_EPS = 0.03
FIX_WIDTH = 0.2
PRODUCE = 0.1355
DESTROY = 3.24

PLANES = 14
OWN = 5
ROWS = 24

MESSAGES = (
    (0, 1, (5, 9), (14, 16), (5, 9), (6, 8)),
    (0, -1, (5, 9), (8, 10), (5, 9), (16, 18)),
    (1, 1, (8, 9), (15, 16), (4, 5), (7, 8)),
    (1, -1, (8, 9), (8, 9), (4, 5), (16, 17)),
    (-1, 1, (5, 6), (15, 16), (9, 10), (7, 8)),
    (-1, -1, (5, 6), (8, 9), (9, 10), (16, 17)),
    (1, 0, (7, 9), (8, 16), (3, 5), (8, 16)),
    (-1, 0, (5, 7), (8, 16), (9, 11), (8, 16)),
)
PACKED = (
    (0, 1, (0, 16)),
    (0, -1, (8, 24)),
    (1, 0, (8, 16)),
    (-1, 0, (8, 16)),
)
FAR, BESIDE = len(MESSAGES), len(PACKED)


def slot(m, c):
    return 2 * (m * 6 + 1 + c)


def across(ref, phase, m, row, first=OWN, count=8):
    return ref.at[pl.ds(((phase * 6 + m) * PLANES + first) * ROWS + row, count, stride=ROWS), :]


def flat(ref):
    return ref.reshape(ref.size // 128, 128)


def conserved(p):
    q = 0.5 * (p[1] * p[1] + p[2] * p[2] + p[3] * p[3])
    return [p[0], p[0] * p[1], p[0] * p[2], p[0] * p[3], 2.5 * p[4] + p[0] * q, p[0] * p[5]]


def primitive(u):
    inv = 1.0 / u[0]
    v = [u[1] * inv, u[2] * inv, u[3] * inv]
    pressure = 0.4 * (u[4] - 0.5 * u[0] * (v[0] * v[0] + v[1] * v[1] + v[2] * v[2]))
    return [u[0], v[0], v[1], v[2], pressure, u[5] * inv]


def reach(*tiles):
    top = low = tiles[0]
    for t in tiles[1:]:
        top, low = jnp.maximum(top, t), jnp.minimum(low, t)
    return top, low


def limit(e, top, low, dc, ap, am, dr):
    da = ap - am
    top, low = jnp.maximum(top, jnp.maximum(ap, am)), jnp.minimum(low, jnp.minimum(ap, am))
    bound = jnp.minimum(top - e, e - low)
    delta = 0.25 * jnp.maximum(jnp.maximum(jnp.abs(dc), jnp.abs(da)), jnp.abs(dr))
    square = bound * bound + LIMIT_EPS
    cross = bound * delta
    factor = jnp.minimum(1.0, (square + 2.0 * cross) / (square + cross + 2.0 * delta * delta))
    quarter = 0.25 * factor
    return (quarter * dc, quarter * da, quarter * dr), (dc, da, dr)


def limit_all(e, cp, cm, ap, am, rp, rm):
    return limit(e, *reach(e, cp, cm, rp, rm), cp - cm, ap, am, rp - rm)


def fix(speed):
    size = jnp.abs(speed)
    return jnp.where(size < FIX_WIDTH, speed * speed * (0.5 / FIX_WIDTH) + 0.5 * FIX_WIDTH, size)


def side(s, d):
    y = lax.rsqrt(s[0])
    root = s[0] * y
    q = 0.5 * (s[1] * s[1] + s[2] * s[2] + s[3] * s[3])
    h = 3.5 * s[4] * (y * y) + q
    m = s[0] * s[d + 1]
    f = [m, m * s[1], m * s[2], m * s[3], m * h, m * s[5]]
    f[d + 1] = f[d + 1] + s[4]
    return root, h, f


def roe(left, right, d):
    rl, hl, fl = side(left, d)
    rr, hr, fr = side(right, d)
    jump = [r - l for l, r in zip(left, right)]
    w = rr / (rl + rr)
    vel = [left[k] + w * jump[k] for k in (1, 2, 3)]
    h = hl + w * (hr - hl)
    nu = left[5] + w * jump[5]
    un = vel[d]
    q = 0.5 * (vel[0] * vel[0] + vel[1] * vel[1] + vel[2] * vel[2])
    c2 = 0.4 * (h - q)
    ic = lax.rsqrt(c2)
    c = c2 * ic
    dens = rl * rr
    x = 0.5 * jump[4] * (ic * ic)
    y = 0.5 * dens * jump[d + 1] * ic
    mid = fix(un)
    slow = fix(un - c) * (x - y)
    fast = fix(un + c) * (x + y)
    both = slow + fast
    wave = mid * (jump[0] - 2.0 * x)
    total = both + wave
    skew = c * (fast - slow)
    shear = mid * dens
    dis = [total]
    inner = None
    for k in range(3):
        if k == d:
            dis.append(total * vel[k] + skew)
        else:
            part = shear * jump[k + 1]
            dis.append(total * vel[k] + part)
            inner = vel[k] * part if inner is None else inner + vel[k] * part
    dis.append(both * h + un * skew + wave * q + inner)
    dis.append(total * nu + shear * jump[5])
    return [fl[k] + fr[k] - dis[k] for k in range(6)]


def kernel(
    flow, inflow, walls, out,
    g, pack, land, packed, top, low, slant, lc, rc, ap, am, rin, rout, src, fa, ns, entry, entry_packed, kinds,
    local_sem, send_sem, recv_sem,
):
    ci, ai, ri = lax.axis_index("circ"), lax.axis_index("axial"), lax.axis_index("rad")
    nc, na = lax.axis_size("circ"), lax.axis_size("axial")
    first, last = ai == 0, ai == na - 1

    def target(dc, da, cross=False):
        return {"circ": lax.rem(ci + dc + nc, nc), "axial": ai + da, "rad": 1 - ri if cross else ri}

    twin = {"circ": ci, "axial": ai, "rad": 1 - ri}

    def guard(da, act):
        if da == 0:
            act()
        else:
            pl.when(ai < na - 1 if da > 0 else ai > 0)(act)

    barrier = pltpu.get_barrier_semaphore()
    for cross, group in ((False, MESSAGES), (True, PACKED)):
        for dc, da, *_ in group:
            guard(da, lambda dc=dc, da=da, cross=cross: pl.semaphore_signal(
                barrier, inc=1, device_id=target(dc, da, cross), device_id_type=MESH))
    pl.semaphore_signal(barrier, inc=1, device_id=twin, device_id_type=MESH)

    load = pltpu.make_async_copy(flow, g.at[0, :, OWN:OWN + 4, 8:16, :], local_sem.at[0])
    load.start()
    kind = pltpu.make_async_copy(walls, kinds, local_sem.at[1])
    kind.start()
    enter = [
        pltpu.make_async_copy(
            inflow.at[:, :, pl.ds(pl.multiple_of(core * 128, 128), 128)], entry.at[k], local_sem.at[2 + k])
        for k, core in enumerate((ri, 1 - ri))
    ]
    for part in enter:
        part.start()

    def remote(phase, k, source, into, device):
        return pltpu.make_async_remote_copy(
            src_ref=source, dst_ref=into, send_sem=send_sem.at[phase, k], recv_sem=recv_sem.at[phase, k],
            device_id=device, device_id_type=MESH,
        )

    def far(phase, k):
        dc, da, sp, sr, tp, tr = MESSAGES[k]
        return remote(
            phase, k, g.at[phase, :, sp[0]:sp[1], sr[0]:sr[1], :], g.at[phase, :, tp[0]:tp[1], tr[0]:tr[1], :],
            target(dc, da))

    def direct(phase, k):
        dc, da, (low, high) = PACKED[k]
        return remote(
            phase, FAR + k, pack.at[phase, low:high, :], land.at[phase, k, low:high, :], target(dc, da, True))

    def own_column(phase):
        return remote(phase, FAR + BESIDE, pack.at[phase, 8:16, :], land.at[phase, BESIDE, 8:16, :], twin)

    def each(group, act, back, along_axis):
        for k, (dc, da, *_) in enumerate(group):
            if (da != 0) == along_axis:
                guard(-da if back else da, lambda k=k: act(k))

    lane = lax.broadcasted_iota(jnp.int32, (8, 128), 1)
    low_rows = lax.broadcasted_iota(jnp.int32, (8, 128), 0) < 4
    at_wall, at_edge = lane == 127 * ri, lane == 127 * (1 - ri)
    inward, outward = jnp.where(ri == 0, 127, 1), jnp.where(ri == 0, 1, 127)
    facing = jnp.where(ri == 0, 1.0, -1.0)
    radial = ri * 128 + lane
    wall_inv = 1.0 / (jnp.minimum(radial, 255 - radial) + 1).astype(jnp.float32)

    def around(e, near, sign):
        inner = pltpu.roll(jnp.where(at_wall, near, e), inward, 1)
        return inner, jnp.where(at_wall, e * sign, pltpu.roll(e, outward, 1))

    def signs(tile):
        return (1.0, tile, tile, -1.0, 1.0, tile)

    def fill(phase):
        tile = jnp.zeros((8, 128), jnp.float32)
        for m in range(6):
            for c in range(4):
                at = slot(m, c)
                e = g[phase, m, OWN + c, 8:16, :]
                turned = pltpu.roll(e, jnp.where(ri == 0, (at + 2) % 128, at), 1)
                tile = jnp.where((lane == at) | (lane == at + 1), turned, tile)
        pack[phase, 8:16, :] = tile
        for row, start in ((15, 0), (8, 20)):
            tile = jnp.zeros((4, 128), jnp.float32)
            for m in range(6):
                e = across(flat(g), phase, m, row, OWN, 4)[...]
                here = lane[0:4] == lax.rem(m + 127 * (1 - ri), 128)
                tile = jnp.where(here, pltpu.roll(e, m, 1) if m else e, tile)
            pack[phase, start:start + 4, :] = tile

    def station_signs():
        for row in range(7, 17):
            station = jnp.clip(ai * 8 + (row - 8), 0, na * 8 - 1)
            value = jnp.where(kinds[ri, station] == 1, -1.0, 1.0)
            ns[pl.ds(row, 1), :] = jnp.full((1, 128), value, jnp.float32)

    def entry_rows():
        row = jnp.zeros((1, 128), jnp.float32)
        for m in range(6):
            for c in range(-1, 5):
                at = lax.rem(ci * 4 + c + nc * 4, nc * 4)
                mine = entry[0, m, pl.ds(at, 1), :]
                for phase in range(2):
                    g[phase, m, OWN + c, 7:8, :] = mine
                if 0 <= c < 4:
                    theirs = entry[1, m, pl.ds(at, 1), :]
                    k = slot(m, c)
                    turned = pltpu.roll(
                        jnp.broadcast_to(theirs, (8, 128)), jnp.where(ri == 0, k, (k + 2) % 128), 1)[0:1]
                    row = jnp.where((lane[0:1] == k) | (lane[0:1] == k + 1), turned, row)
        entry_packed[0:1, :] = row

    def section(phase, carry):
        each(MESSAGES, lambda k: far(phase, k).start(), False, True)
        each(PACKED, lambda k: direct(phase, k).start(), False, True)
        own_column(phase).start()
        each(PACKED, lambda k: direct(phase, k).start(), False, False)
        each(MESSAGES, lambda k: far(phase, k).start(), False, False)

        def cell(m, c):
            return g[phase, m, OWN + c, 8:16, :]

        def turned(tile):
            return pltpu.roll(tile, jnp.where(ri == 0, 0, 126), 1)

        tile_sign = signs(ns[8:16, :])

        def prepare(c, columns, shift):
            for m in range(6):
                e = cell(m, c)
                inner, outer = around(e, pltpu.roll(columns, (128 - slot(m, shift)) % 128, 1), tile_sign[m])
                top[m, c + 1], low[m, c + 1] = reach(e, cell(m, c + 1), cell(m, c - 1), inner, outer)
                slant[m, c + 1] = inner - outer

        own_column(phase).wait_recv()
        each(MESSAGES, lambda k: far(phase, k).wait_recv(), True, False)
        ours = turned(land[phase, BESIDE, 8:16, :])
        for c in range(4):
            prepare(c, ours, c)
        each(PACKED, lambda k: direct(phase, k).wait_recv(), True, False)
        prepare(-1, turned(land[phase, 2, 8:16, :]), 3)
        prepare(4, turned(land[phase, 3, 8:16, :]), 0)

        each(MESSAGES, lambda k: far(phase, k).wait_recv(), True, True)

        @pl.when(last)
        def _():
            for m in range(6):
                for plane in range(OWN - 1, OWN + 5):
                    g[phase, m, plane, 16:17, :] = g[phase, m, plane, 15:16, :]

        def slopes(m, c):
            e = cell(m, c)
            return e, *limit(
                e, top[m, c + 1], low[m, c + 1], cell(m, c + 1) - cell(m, c - 1),
                g[phase, m, OWN + c, 9:17, :], g[phase, m, OWN + c, 7:15, :], slant[m, c + 1])

        def circ_face(c):
            return roe([lc[m, c] for m in range(6)], [rc[m, c + 1] for m in range(6)], 0)

        for c in range(4):
            diffs = []
            for m in range(6):
                e, hs, diff = slopes(m, c)
                diffs.append(diff)
                lc[m, c + 1] = e + hs[0]
                rc[m, c + 1] = e - hs[0]
                ap[m, OWN + c, 8:16, :] = e + hs[1]
                am[m, OWN + c, 8:16, :] = e - hs[1]
                scale = facing if m == 3 else 1.0
                rin[m, c] = (e + hs[2]) * scale
                rout[m, c] = (e - hs[2]) * scale
            oc = diffs[3][1] - diffs[2][2] * facing
            oa = diffs[1][2] * facing - diffs[3][0]
            orr = diffs[2][0] - diffs[1][1]
            s = jnp.sqrt(oc * oc + oa * oa + orr * orr)
            dens, nu = cell(0, c), cell(5, c)
            ratio = nu * wall_inv
            src[c] = (0.5 * PRODUCE) * s * dens * nu - DESTROY * dens * (ratio * ratio)

        radial_faces = []
        for c in range(4):
            ghost = [cell(m, c) * tile_sign[m] for m in range(6)]
            ghost[3] = ghost[3] * facing
            left = [jnp.where(at_wall, ghost[m], pltpu.roll(rin[m, c], outward, 1)) for m in range(6)]
            radial_faces.append(roe(left, [rout[m, c] for m in range(6)], 2))
        circ_faces = [None] + [circ_face(c) for c in range(1, 4)] + [None]


        for m in range(6):
            e, hs, _ = slopes(m, -1)
            lc[m, 0] = e + hs[0]
            e, hs, _ = slopes(m, 4)
            rc[m, 5] = e - hs[0]
        circ_faces[0], circ_faces[4] = circ_face(0), circ_face(4)

        each(PACKED, lambda k: direct(phase, k).wait_recv(), True, True)

        g_f, ap_f, am_f, fa_f = flat(g), flat(ap), flat(am), flat(fa)

        def both(m, step_row, step_plane):
            return jnp.where(
                low_rows,
                across(g_f, phase, m, 7 + step_row, OWN + step_plane)[...],
                across(g_f, phase, m, 16 + step_row, OWN - 4 + step_plane)[...])

        row_sign = signs(jnp.where(
            low_rows, jnp.broadcast_to(ns[7:8, :], (8, 128)), jnp.broadcast_to(ns[16:17, :], (8, 128))))
        columns = jnp.where(low_rows, land[phase, 0, 0:8, :], land[phase, 1, 16:24, :])
        outside = (low_rows & first) | (jnp.logical_not(low_rows) & last)
        for m in range(6):
            e = both(m, 0, 0)
            inner, outer = around(e, pltpu.roll(columns, 128 - m, 1) if m else columns, row_sign[m])
            hs, _ = limit_all(e, both(m, 0, 1), both(m, 0, -1), both(m, 1, 0), both(m, -1, 0), inner, outer)
            slope = jnp.where(outside, 0.0, hs[1])
            across(ap_f, 0, m, 7, OWN)[...] = e + slope
            across(am_f, 0, m, 16, OWN - 4)[...] = e - slope

        place = lax.rem(lane // 2, 6)
        halo = jnp.where(place == 0, pltpu.roll(land[phase, 2, 8:16, :], 120, 1), land[phase, BESIDE, 8:16, :])
        halo = jnp.where(place == 5, pltpu.roll(land[phase, 3, 8:16, :], 8, 1), halo)
        packed[8:16, :] = halo
        packed[7:8, :] = jnp.where(first, entry_packed[0:1, :], land[phase, 0, 15:16, :])
        packed[16:17, :] = jnp.where(last, packed[15:16, :], land[phase, 1, 8:9, :])
        beyond, mine = pltpu.roll(halo, inward, 1), pltpu.roll(pack[phase, 8:16, :], inward, 1)
        hs, _ = limit_all(
            halo, pltpu.roll(halo, 126, 1), pltpu.roll(halo, 2, 1), packed[9:17, :], packed[7:15, :], beyond, mine
        )
        near_face = halo - hs[2]

        left, right = [], []
        for m in range(6):
            tile = rin[m, 0]
            for c in range(1, 4):
                tile = jnp.where(at_edge, rin[m, c], pltpu.roll(tile, 126, 1))
            left.append(tile)
            right.append(pltpu.roll(near_face, (121 - slot(m, 0)) % 128, 1))
        right[3] = right[3] * facing
        middle = roe(left, right, 2)

        for c in range(4):
            f = roe([ap[m, OWN + c, 7:15, :] for m in range(6)], [am[m, OWN + c, 8:16, :] for m in range(6)], 1)
            for m in range(6):
                fa[m, OWN + c, 8:16, :] = f[m]
        f = roe([across(ap_f, 0, m, 15)[...] for m in range(6)], [across(am_f, 0, m, 16)[...] for m in range(6)], 1)
        for m in range(6):
            across(fa_f, 0, m, 16)[...] = f[m]
        for c in range(4):
            u0 = conserved([cell(m, c) for m in range(6)])
            u1 = []
            for m in range(6):
                face = radial_faces[c][m]
                inner = jnp.where(
                    at_edge, pltpu.roll(middle[m], 6 - 2 * c, 1) if c < 3 else middle[m], pltpu.roll(face, inward, 1))
                along = inner - face
                if m == 3:
                    along = along * facing
                total = (
                    (circ_faces[c + 1][m] - circ_faces[c][m])
                    + (fa[m, OWN + c, 9:17, :] - fa[m, OWN + c, 8:16, :])
                    + along
                )
                change = (-0.5 * STEP_SIZE) * total
                if m == 5:
                    change = change + STEP_SIZE * src[c]
                u1.append(u0[m] + change)
                out[m, c] = jnp.where(phase == 0, u0[m], out[m, c]) + 0.5 * change
            w = primitive(u1)
            for m in range(6):
                g[phase + 1, m, OWN + c, 8:16, :] = w[m]
        fill(phase + 1)
        return carry

    load.wait()
    kind.wait()
    for part in enter:
        part.wait()
    station_signs()
    pl.when(first)(entry_rows)
    fill(0)
    pl.semaphore_wait(barrier, FAR + BESIDE + 1 - 4 * first.astype(jnp.int32) - 4 * last.astype(jnp.int32))
    lax.fori_loop(0, 2, section, 0)
    for phase in range(2):
        own_column(phase).wait_send()
        for along_axis in (True, False):
            each(MESSAGES, lambda k: far(phase, k).wait_send(), False, along_axis)
            each(PACKED, lambda k: direct(phase, k).wait_send(), False, along_axis)


def solution(mesh):
    def vmem(*shape):
        return pltpu.VMEM(shape, jnp.float32)

    def body(flow, inflow, wall_kind):
        padded = (6, PLANES, ROWS, 128)
        tiles = (6, 6, 8, 128)
        inner = (6, 4, 8, 128)
        copies = FAR + BESIDE + 1
        return pl.pallas_call(
            kernel,
            out_shape=pltpu.VMEM(flow.shape, jnp.float32),
            in_specs=[pl.BlockSpec(memory_space=pl.ANY)] * 3,
            out_specs=pl.BlockSpec(memory_space=pltpu.VMEM),
            scratch_shapes=[
                vmem(3, *padded), vmem(3, 24, 128), vmem(2, BESIDE + 1, 24, 128),
                vmem(24, 128), vmem(*tiles), vmem(*tiles), vmem(*tiles), vmem(*tiles), vmem(*tiles), vmem(*padded), vmem(*padded), vmem(*inner), vmem(*inner),
                vmem(4, 8, 128), vmem(*padded), vmem(ROWS, 128), vmem(2, 6, inflow.shape[1], 128), vmem(8, 128),
                pltpu.SMEM((2, wall_kind.shape[0]), jnp.int32),
                pltpu.SemaphoreType.DMA((4,)),
                pltpu.SemaphoreType.DMA((2, copies)), pltpu.SemaphoreType.DMA((2, copies)),
            ],
            compiler_params=pltpu.CompilerParams(
                collective_id=0, has_side_effects=True, vmem_limit_bytes=56 * 2**20
            ),
        )(flow, inflow, wall_kind.T)

    spec = P(None, "circ", "axial", "rad")
    return jax.shard_map(body, mesh=mesh, in_specs=(spec, P(), P()), out_specs=spec, check_vma=False)
```

time: 29.6 us -> 27.9 us (0.943)
  Pallas kernels: 28.8 us -> 27.1 us
    pallas_call x1, Pallas kernels: 28.8 us -> 27.1 us  [body(): pl.pallas_call(kernel, out_shape=pltpu.VMEM(flow.shape, jnp.float32), in_...]
where the time goes in v4:
time: 27.9 us; the launch traced here: 27.8 us
  Pallas kernels  27.1 us (97%)
  local copies, waits for them, and re-layouts  0.64 us (2%)
    pallas_call x1, Pallas kernels, body(): pl.pallas_call(kernel, out_shape=pltpu.VMEM(flow.shape, jnp.float32), in_...  27.1 us
    unnamed x1, local copies, waits for them, and re-layouts  0.64 us

profile of v4, /device:TPU:1, one launch (start us, length us, event | category | flops | bytes accessed | tf_op | source)
XLA Modules:
  0.0 27.8 jit_solution(11150331076100837583)
XLA Ops:
  0.0 27.1 %shard_map.37 = f32[6,4,8,128]{3,2,1,0:T(8,128)S(1)} custom-call(f32[6,4,8,128]{3,2,1,0:T(8,128)} %flow.1, f32[6,64,256]{2,1,0:T(8,128)} %inflow.1, s32[2,192]{1,0:T(2,128)} %bitcast.1), custom_call_target="tpu_custom_call" | custom-call | tf_op jit(solution)/shard_map/pallas_call | solution.py:443
  27.1 0.6 %copy.5 = f32[6,4,8,128]{3,2,1,0:T(8,128)} copy(f32[6,4,8,128]{3,2,1,0:T(8,128)S(1)} %shard_map.37) | data formatting | bytes 196608

commit v5 on v4

--- a/solution.py
+++ b/solution.py
@@ -256,10 +256,23 @@
 
     def section(phase, carry):
         each(MESSAGES, lambda k: far(phase, k).start(), False, True)
+
+        @pl.when(phase > 0)
+        def _():
+            fill(phase)
+
+        own_column(phase).start()
         each(PACKED, lambda k: direct(phase, k).start(), False, True)
-        own_column(phase).start()
         each(PACKED, lambda k: direct(phase, k).start(), False, False)
         each(MESSAGES, lambda k: far(phase, k).start(), False, False)
+
+        @pl.when(phase == 0)
+        def _():
+            kind.wait()
+            for part in enter:
+                part.wait()
+            station_signs()
+            pl.when(first)(entry_rows)
 
         def cell(m, c):
             return g[phase, m, OWN + c, 8:16, :]
@@ -281,9 +294,6 @@
         ours = turned(land[phase, BESIDE, 8:16, :])
         for c in range(4):
             prepare(c, ours, c)
-        each(PACKED, lambda k: direct(phase, k).wait_recv(), True, False)
-        prepare(-1, turned(land[phase, 2, 8:16, :]), 3)
-        prepare(4, turned(land[phase, 3, 8:16, :]), 0)
 
         each(MESSAGES, lambda k: far(phase, k).wait_recv(), True, True)
 
@@ -331,12 +341,37 @@
         circ_faces = [None] + [circ_face(c) for c in range(1, 4)] + [None]
 
 
+        each(PACKED, lambda k: direct(phase, k).wait_recv(), True, False)
+        prepare(-1, turned(land[phase, 2, 8:16, :]), 3)
+        prepare(4, turned(land[phase, 3, 8:16, :]), 0)
+
         for m in range(6):
             e, hs, _ = slopes(m, -1)
             lc[m, 0] = e + hs[0]
             e, hs, _ = slopes(m, 4)
             rc[m, 5] = e - hs[0]
         circ_faces[0], circ_faces[4] = circ_face(0), circ_face(4)
+
+        for c in range(4):
+            f = roe([ap[m, OWN + c, 7:15, :] for m in range(6)], [am[m, OWN + c, 8:16, :] for m in range(6)], 1)
+            for m in range(6):
+                fa[m, OWN + c, 8:16, :] = f[m]
+
+        before, starts, inners = [], [], []
+        for c in range(4):
+            starts.append(conserved([cell(m, c) for m in range(6)]))
+            before.append([])
+            inners.append([])
+            for m in range(6):
+                face = radial_faces[c][m] * facing if m == 3 else radial_faces[c][m]
+                inners[c].append(pltpu.roll(face, inward, 1))
+                before[c].append((circ_faces[c + 1][m] - circ_faces[c][m]) - face)
+        left = []
+        for m in range(6):
+            tile = rin[m, 0]
+            for c in range(1, 4):
+                tile = jnp.where(at_edge, rin[m, c], pltpu.roll(tile, 126, 1))
+            left.append(tile)
 
         each(PACKED, lambda k: direct(phase, k).wait_recv(), True, True)
 
@@ -372,38 +407,24 @@
         )
         near_face = halo - hs[2]
 
-        left, right = [], []
-        for m in range(6):
-            tile = rin[m, 0]
-            for c in range(1, 4):
-                tile = jnp.where(at_edge, rin[m, c], pltpu.roll(tile, 126, 1))
-            left.append(tile)
-            right.append(pltpu.roll(near_face, (121 - slot(m, 0)) % 128, 1))
+        right = [pltpu.roll(near_face, (121 - slot(m, 0)) % 128, 1) for m in range(6)]
         right[3] = right[3] * facing
         middle = roe(left, right, 2)
-
-        for c in range(4):
-            f = roe([ap[m, OWN + c, 7:15, :] for m in range(6)], [am[m, OWN + c, 8:16, :] for m in range(6)], 1)
-            for m in range(6):
-                fa[m, OWN + c, 8:16, :] = f[m]
-        f = roe([across(ap_f, 0, m, 15)[...] for m in range(6)], [across(am_f, 0, m, 16)[...] for m in range(6)], 1)
-        for m in range(6):
-            across(fa_f, 0, m, 16)[...] = f[m]
-        for c in range(4):
-            u0 = conserved([cell(m, c) for m in range(6)])
-            u1 = []
-            for m in range(6):
-                face = radial_faces[c][m]
-                inner = jnp.where(
-                    at_edge, pltpu.roll(middle[m], 6 - 2 * c, 1) if c < 3 else middle[m], pltpu.roll(face, inward, 1))
-                along = inner - face
-                if m == 3:
-                    along = along * facing
-                total = (
-                    (circ_faces[c + 1][m] - circ_faces[c][m])
-                    + (fa[m, OWN + c, 9:17, :] - fa[m, OWN + c, 8:16, :])
-                    + along
-                )
+        middle[3] = middle[3] * facing
+
+        ends = roe(
+            [jnp.where(low_rows, across(ap_f, 0, m, 7)[...], across(ap_f, 0, m, 15, OWN - 4)[...]) for m in range(6)],
+            [jnp.where(low_rows, across(am_f, 0, m, 8)[...], across(am_f, 0, m, 16, OWN - 4)[...]) for m in range(6)],
+            1)
+        for m in range(6):
+            across(fa_f, 0, m, 8, OWN, 4)[...] = ends[m][0:4]
+            across(fa_f, 0, m, 16, OWN - 4)[...] = ends[m]
+
+        for c in range(4):
+            u0, u1 = starts[c], []
+            for m in range(6):
+                inner = jnp.where(at_edge, pltpu.roll(middle[m], 6 - 2 * c, 1) if c < 3 else middle[m], inners[c][m])
+                total = before[c][m] + inner + (fa[m, OWN + c, 9:17, :] - fa[m, OWN + c, 8:16, :])
                 change = (-0.5 * STEP_SIZE) * total
                 if m == 5:
                     change = change + STEP_SIZE * src[c]
@@ -412,15 +433,9 @@
             w = primitive(u1)
             for m in range(6):
                 g[phase + 1, m, OWN + c, 8:16, :] = w[m]
-        fill(phase + 1)
         return carry
 
     load.wait()
-    kind.wait()
-    for part in enter:
-        part.wait()
-    station_signs()
-    pl.when(first)(entry_rows)
     fill(0)
     pl.semaphore_wait(barrier, FAR + BESIDE + 1 - 4 * first.astype(jnp.int32) - 4 * last.astype(jnp.int32))
     lax.fori_loop(0, 2, section, 0)
@@ -446,7 +461,7 @@
             in_specs=[pl.BlockSpec(memory_space=pl.ANY)] * 3,
             out_specs=pl.BlockSpec(memory_space=pltpu.VMEM),
             scratch_shapes=[
-                vmem(3, *padded), vmem(3, 24, 128), vmem(2, BESIDE + 1, 24, 128),
+                vmem(3, *padded), vmem(2, 24, 128), vmem(2, BESIDE + 1, 24, 128),
                 vmem(24, 128), vmem(*tiles), vmem(*tiles), vmem(*tiles), vmem(*tiles), vmem(*tiles), vmem(*padded), vmem(*padded), vmem(*inner), vmem(*inner),
                 vmem(4, 8, 128), vmem(*padded), vmem(ROWS, 128), vmem(2, 6, inflow.shape[1], 128), vmem(8, 128),
                 pltpu.SMEM((2, wall_kind.shape[0]), jnp.int32),

time: 27.9 us -> 27.4 us (0.982)
  the two profiles are of different devices: /device:TPU:1 before, /device:TPU:512 now
where the time goes in v5:
time: 27.4 us; the launch traced here: 27.3 us
  Pallas kernels  26.6 us (97%)
  local copies, waits for them, and re-layouts  0.64 us (2%)
    pallas_call x1, Pallas kernels, body(): pl.pallas_call(kernel, out_shape=pltpu.VMEM(flow.shape, jnp.float32), in_...  26.6 us
    unnamed x1, local copies, waits for them, and re-layouts  0.64 us

profile of v5, /device:TPU:512, one launch (start us, length us, event | category | flops | bytes accessed | tf_op | source)
XLA Modules:
  0.0 27.3 jit_solution(9300648859624445430)
XLA Ops:
  0.0 26.6 %shard_map.37 = f32[6,4,8,128]{3,2,1,0:T(8,128)S(1)} custom-call(f32[6,4,8,128]{3,2,1,0:T(8,128)} %flow.1, f32[6,64,256]{2,1,0:T(8,128)} %inflow.1, s32[2,192]{1,0:T(2,128)} %bitcast.1), custom_call_target="tpu_custom_call" | custom-call | tf_op jit(solution)/shard_map/pallas_call | solution.py:458
  26.6 0.6 %copy.5 = f32[6,4,8,128]{3,2,1,0:T(8,128)} copy(f32[6,4,8,128]{3,2,1,0:T(8,128)S(1)} %shard_map.37) | data formatting | bytes 196608

commit v6 on v5

--- a/solution.py
+++ b/solution.py
@@ -27,8 +27,8 @@
     (-1, 0, (5, 7), (8, 16), (9, 11), (8, 16)),
 )
 PACKED = (
-    (0, 1, (0, 16)),
-    (0, -1, (8, 24)),
+    (0, 1, (15, 20)),
+    (0, -1, (4, 9)),
     (1, 0, (8, 16)),
     (-1, 0, (8, 16)),
 )
@@ -195,9 +195,9 @@
     def own_column(phase):
         return remote(phase, FAR + BESIDE, pack.at[phase, 8:16, :], land.at[phase, BESIDE, 8:16, :], twin)
 
-    def each(group, act, back, along_axis):
+    def each(group, act, back, kind):
         for k, (dc, da, *_) in enumerate(group):
-            if (da != 0) == along_axis:
+            if kind in ("all", ("circ", "axial", "corner")[(da != 0) + (dc != 0 and da != 0)]):
                 guard(-da if back else da, lambda k=k: act(k))
 
     lane = lax.broadcasted_iota(jnp.int32, (8, 128), 1)
@@ -224,7 +224,7 @@
                 turned = pltpu.roll(e, jnp.where(ri == 0, (at + 2) % 128, at), 1)
                 tile = jnp.where((lane == at) | (lane == at + 1), turned, tile)
         pack[phase, 8:16, :] = tile
-        for row, start in ((15, 0), (8, 20)):
+        for row, start in ((15, 16), (8, 4)):
             tile = jnp.zeros((4, 128), jnp.float32)
             for m in range(6):
                 e = across(flat(g), phase, m, row, OWN, 4)[...]
@@ -255,16 +255,17 @@
         entry_packed[0:1, :] = row
 
     def section(phase, carry):
-        each(MESSAGES, lambda k: far(phase, k).start(), False, True)
+        each(MESSAGES, lambda k: far(phase, k).start(), False, "axial")
 
         @pl.when(phase > 0)
         def _():
             fill(phase)
 
+        each(PACKED, lambda k: direct(phase, k).start(), False, "axial")
+        each(MESSAGES, lambda k: far(phase, k).start(), False, "corner")
         own_column(phase).start()
-        each(PACKED, lambda k: direct(phase, k).start(), False, True)
-        each(PACKED, lambda k: direct(phase, k).start(), False, False)
-        each(MESSAGES, lambda k: far(phase, k).start(), False, False)
+        each(PACKED, lambda k: direct(phase, k).start(), False, "circ")
+        each(MESSAGES, lambda k: far(phase, k).start(), False, "circ")
 
         @pl.when(phase == 0)
         def _():
@@ -290,12 +291,12 @@
                 slant[m, c + 1] = inner - outer
 
         own_column(phase).wait_recv()
-        each(MESSAGES, lambda k: far(phase, k).wait_recv(), True, False)
+        each(MESSAGES, lambda k: far(phase, k).wait_recv(), True, "circ")
         ours = turned(land[phase, BESIDE, 8:16, :])
         for c in range(4):
             prepare(c, ours, c)
 
-        each(MESSAGES, lambda k: far(phase, k).wait_recv(), True, True)
+        each(MESSAGES, lambda k: far(phase, k).wait_recv(), True, "axial")
 
         @pl.when(last)
         def _():
@@ -341,7 +342,8 @@
         circ_faces = [None] + [circ_face(c) for c in range(1, 4)] + [None]
 
 
-        each(PACKED, lambda k: direct(phase, k).wait_recv(), True, False)
+        each(PACKED, lambda k: direct(phase, k).wait_recv(), True, "circ")
+        each(MESSAGES, lambda k: far(phase, k).wait_recv(), True, "corner")
         prepare(-1, turned(land[phase, 2, 8:16, :]), 3)
         prepare(4, turned(land[phase, 3, 8:16, :]), 0)
 
@@ -373,7 +375,7 @@
                 tile = jnp.where(at_edge, rin[m, c], pltpu.roll(tile, 126, 1))
             left.append(tile)
 
-        each(PACKED, lambda k: direct(phase, k).wait_recv(), True, True)
+        each(PACKED, lambda k: direct(phase, k).wait_recv(), True, "axial")
 
         g_f, ap_f, am_f, fa_f = flat(g), flat(ap), flat(am), flat(fa)
 
@@ -385,7 +387,7 @@
 
         row_sign = signs(jnp.where(
             low_rows, jnp.broadcast_to(ns[7:8, :], (8, 128)), jnp.broadcast_to(ns[16:17, :], (8, 128))))
-        columns = jnp.where(low_rows, land[phase, 0, 0:8, :], land[phase, 1, 16:24, :])
+        columns = jnp.where(low_rows, land[phase, 0, 16:24, :], land[phase, 1, 0:8, :])
         outside = (low_rows & first) | (jnp.logical_not(low_rows) & last)
         for m in range(6):
             e = both(m, 0, 0)
@@ -441,9 +443,8 @@
     lax.fori_loop(0, 2, section, 0)
     for phase in range(2):
         own_column(phase).wait_send()
-        for along_axis in (True, False):
-            each(MESSAGES, lambda k: far(phase, k).wait_send(), False, along_axis)
-            each(PACKED, lambda k: direct(phase, k).wait_send(), False, along_axis)
+        each(MESSAGES, lambda k: far(phase, k).wait_send(), False, "all")
+        each(PACKED, lambda k: direct(phase, k).wait_send(), False, "all")
 
 
 def solution(mesh):

time: 27.4 us -> 26.8 us (0.978)
  the two profiles are of different devices: /device:TPU:512 before, /device:TPU:1 now
where the time goes in v6:
time: 26.8 us; the launch traced here: 26.7 us
  Pallas kernels  26 us (97%)
  local copies, waits for them, and re-layouts  0.64 us (2%)
    pallas_call x1, Pallas kernels, body(): pl.pallas_call(kernel, out_shape=pltpu.VMEM(flow.shape, jnp.float32), in_...  26 us
    unnamed x1, local copies, waits for them, and re-layouts  0.64 us

profile of v6, /device:TPU:1, one launch (start us, length us, event | category | flops | bytes accessed | tf_op | source)
XLA Modules:
  0.0 26.7 jit_solution(14749467692559733329)
XLA Ops:
  0.0 26.0 %shard_map.37 = f32[6,4,8,128]{3,2,1,0:T(8,128)S(1)} custom-call(f32[6,4,8,128]{3,2,1,0:T(8,128)} %flow.1, f32[6,64,256]{2,1,0:T(8,128)} %inflow.1, s32[2,192]{1,0:T(2,128)} %bitcast.1), custom_call_target="tpu_custom_call" | custom-call | tf_op jit(solution)/shard_map/pallas_call | solution.py:459
  26.0 0.6 %copy.5 = f32[6,4,8,128]{3,2,1,0:T(8,128)} copy(f32[6,4,8,128]{3,2,1,0:T(8,128)S(1)} %shard_map.37) | data formatting | bytes 196608

commit v7 on v6

--- a/solution.py
+++ b/solution.py
@@ -431,16 +431,18 @@
                 if m == 5:
                     change = change + STEP_SIZE * src[c]
                 u1.append(u0[m] + change)
-                out[m, c] = jnp.where(phase == 0, u0[m], out[m, c]) + 0.5 * change
-            w = primitive(u1)
-            for m in range(6):
-                g[phase + 1, m, OWN + c, 8:16, :] = w[m]
+                out[m, c] = (u0[m] if phase == 0 else out[m, c]) + 0.5 * change
+            if phase == 0:
+                w = primitive(u1)
+                for m in range(6):
+                    g[1, m, OWN + c, 8:16, :] = w[m]
         return carry
 
     load.wait()
     fill(0)
     pl.semaphore_wait(barrier, FAR + BESIDE + 1 - 4 * first.astype(jnp.int32) - 4 * last.astype(jnp.int32))
-    lax.fori_loop(0, 2, section, 0)
+    for phase in range(2):
+        section(phase, 0)
     for phase in range(2):
         own_column(phase).wait_send()
         each(MESSAGES, lambda k: far(phase, k).wait_send(), False, "all")

time: 26.8 us -> 26.8 us (level)
  no operation moved by 1% of the time
where the time goes in v7:
time: 26.8 us; the launch traced here: 26.6 us
  Pallas kernels  26 us (97%)
  local copies, waits for them, and re-layouts  0.64 us (2%)
    pallas_call x1, Pallas kernels, body(): pl.pallas_call(kernel, out_shape=pltpu.VMEM(flow.shape, jnp.float32), in_...  26 us
    unnamed x1, local copies, waits for them, and re-layouts  0.64 us

profile of v7, /device:TPU:1, one launch (start us, length us, event | category | flops | bytes accessed | tf_op | source)
XLA Modules:
  0.0 26.6 jit_solution(3836249248154028491)
XLA Ops:
  0.0 26.0 %shard_map.37 = f32[6,4,8,128]{3,2,1,0:T(8,128)S(1)} custom-call(f32[6,4,8,128]{3,2,1,0:T(8,128)} %flow.1, f32[6,64,256]{2,1,0:T(8,128)} %inflow.1, s32[2,192]{1,0:T(2,128)} %bitcast.1), custom_call_target="tpu_custom_call" | custom-call | tf_op jit(solution)/shard_map/pallas_call | solution.py:461
  26.0 0.6 %copy.5 = f32[6,4,8,128]{3,2,1,0:T(8,128)} copy(f32[6,4,8,128]{3,2,1,0:T(8,128)S(1)} %shard_map.37) | data formatting | bytes 196608
